TPU v7x, 128 devices: a whole 4x4x4 slice. The times are simulated.
128 devices in a mesh: face: 8 (over y_lo, x), row: 16 (over y_hi, z, core).
Axes of the slice: x: 4, y: 4 (y_hi: 2, y_lo: 2; y = y_hi * 2 + y_lo), z: 4, core: 2. Of those that a mesh axis runs over, the one named last changes fastest.
Arguments:
- state_field: bfloat16 [8, 256, 256, 128], P('face', 'row'), may hold values from -6 to 6
- adjacency: int32 [2, 8, 4], replicated, may hold values from 0 to 7, as said below
- edge_flips: int32 [8, 2], replicated, may hold values from 0 to 1, as said below
- conv_first: bfloat16 [3, 3, 128, 128], replicated, may hold values from -0.1875 to 0.1875
- bias_first: float32 [128], replicated, may hold values from -3 to 3
- conv_second: bfloat16 [3, 3, 128, 128], replicated, may hold values from -0.1875 to 0.1875
- bias_second: float32 [128], replicated, may hold values from -3 to 3
- norm_gain: float32 [128], replicated, may hold values from 0.1 to 1.9
- up_weight: bfloat16 [128, 512], replicated, may hold values from -0.5 to 0.5
- up_bias: float32 [512], replicated, may hold values from -3 to 3
- down_weight: bfloat16 [512, 128], replicated, may hold values from -0.25 to 0.25
- down_bias: float32 [128], replicated, may hold values from -3 to 3
Outputs:
- block_out: bfloat16 [8, 256, 256, 128], P('face', 'row')
Inputs may be any that keep to these rules, and one draw needn't show every extreme that they name: adjacency[0, f, e] is the face across edge e of face f and adjacency[1, f, e] the edge of that face that it meets; row edges (0, 1) meet row edges and column edges (2, 3) meet column edges; the pairing is mutual, every edge of every face in exactly one pair; column edges meet in the same order. `edge_flips`: equal for the two edges of a pair.
All inputs are finite; a program needn't handle non-finite values.
Results may differ from a plain program's by a relative error of at most 0.0045.
Values may be sent and summed in bfloat16 or wider, within the bound.
A program may use at most 64 MiB of HBM per device.

v0:
```python
import jax
import jax.numpy as jnp
from jax import lax
from jax.sharding import PartitionSpec as P


def extended(value, sides, width):
    for axis, dim in sides:
        size, length = (lax.axis_size(axis), value.shape[dim])
        up = [(i, (i + 1) % size) for i in range(size)]
        down = [(j, i) for i, j in up]
        last = lax.slice_in_dim(value, length - width, length, axis=dim)
        initial = lax.slice_in_dim(value, 0, width, axis=dim)
        before = lax.ppermute(last, axis, up)
        after = lax.ppermute(initial, axis, down)
        value = jnp.concatenate([before, value, after], axis=dim)
    return value


def gelu_exact(values):
    return jax.nn.gelu(values, approximate=False)


def convolve_padded(padded, kernel):
    row_count = padded.shape[0] - 2
    col_count = padded.shape[1] - 2
    chan_count = kernel.shape[3]
    summed = jnp.zeros((row_count * col_count, chan_count), jnp.float32)
    for row_step in range(3):
        for col_step in range(3):
            window = padded[row_step : row_step + row_count, col_step : col_step + col_count]
            window = window.reshape(row_count * col_count, -1)
            summed = summed + jnp.dot(
                window, kernel[row_step, col_step], preferred_element_type=jnp.float32
            )
    return summed.reshape(row_count, col_count, chan_count)


def mixer(second_sum, residual, norm_gain, up_weight, up_bias, down_weight, down_bias):
    row_count, col_count, chan_count = second_sum.shape
    pixels = row_count * col_count
    blocks = max(1, pixels // 4096)
    while pixels % blocks:
        blocks = blocks - 1
    flat_rows = second_sum.reshape(blocks, pixels // blocks, chan_count)
    flat_skip = residual.reshape(blocks, pixels // blocks, chan_count)

    def mix_block(members):
        block_rows, skip_rows = members
        centre = block_rows - jnp.mean(block_rows, -1, keepdims=True)
        spread = jnp.mean(centre * centre, -1, keepdims=True)
        normed = (centre * lax.rsqrt(spread + 1e-06) * norm_gain).astype(jnp.bfloat16)
        hidden_act = gelu_exact(
            jnp.dot(normed, up_weight, preferred_element_type=jnp.float32) + up_bias
        ).astype(jnp.bfloat16)
        projected = jnp.dot(hidden_act, down_weight, preferred_element_type=jnp.float32) + down_bias
        return (skip_rows.astype(jnp.float32) + projected).astype(jnp.bfloat16)

    return lax.map(mix_block, (flat_rows, flat_skip)).reshape(row_count, col_count, chan_count)


def pick_edges(gathered, targets):
    item_count = gathered.shape[0]
    onehot = (jnp.arange(item_count, dtype=jnp.int32)[None, :] == targets[:, None]).astype(
        jnp.bfloat16
    )
    flat_edges = gathered.reshape(item_count, -1)
    chosen = jnp.dot(onehot, flat_edges, preferred_element_type=jnp.float32)
    return chosen.astype(jnp.bfloat16).reshape((targets.shape[0],) + gathered.shape[1:])


def gather_rims(block, adjacency, edge_flips):
    row_count, col_count, chan_count = block.shape
    row_devices = lax.axis_size("row")
    row_index = lax.axis_index("row")
    face_index = lax.axis_index("face")
    at_first = row_index == 0
    at_last = row_index == row_devices - 1
    face_table = lax.dynamic_index_in_dim(adjacency, face_index, 1, keepdims=False)
    flip_pair = lax.dynamic_index_in_dim(edge_flips, face_index, 0, keepdims=False)
    row_targets = face_table[0, 0:2] * 2 + face_table[1, 0:2]
    col_targets = face_table[0, 2:4] * 2 + face_table[1, 2:4] - 2
    padded = extended(block, (("row", 0),), 1)
    columns = jnp.stack([padded[:, 0], padded[:, col_count - 1]])
    end_rows = jnp.stack([block[0], block[row_count - 1]])
    spread = lax.all_to_all(end_rows, "row", split_axis=1, concat_axis=0, tiled=True)
    own_pieces = jnp.stack([spread[0], spread[2 * row_devices - 1]])
    row_gathered, col_gathered = (
        lax.all_gather(own_pieces, "face", axis=0, tiled=True),
        lax.all_gather(columns, "face", axis=0, tiled=True),
    )
    edge_pieces = pick_edges(row_gathered, row_targets)
    beyond_rows = lax.all_gather(edge_pieces, "row", axis=1, tiled=True)
    beyond_rows = jnp.where(flip_pair[:, None, None] == 1, beyond_rows[:, ::-1], beyond_rows)
    side_cols = pick_edges(col_gathered, col_targets)
    positions = jnp.arange(row_count + 2, dtype=jnp.int32)
    corner_mask = (positions == 0) & at_first | (positions == row_count + 1) & at_last
    side_cols = jnp.where(corner_mask[None, :, None], jnp.zeros((), jnp.bfloat16), side_cols)
    upper_row = jnp.where(at_first, beyond_rows[0], padded[0])
    lower_row = jnp.where(at_last, beyond_rows[1], padded[row_count + 1])
    return (padded, upper_row, lower_row, side_cols)


def convolve(block, kernel, adjacency, edge_flips):
    row_count, col_count, chan_count = block.shape
    padded, upper_row, lower_row, side_cols = gather_rims(block, adjacency, edge_flips)
    middle = jnp.concatenate([upper_row[None], padded[1 : row_count + 1], lower_row[None]], 0)
    assembled = jnp.concatenate([side_cols[0][:, None], middle, side_cols[1][:, None]], 1)
    return convolve_padded(assembled, kernel)


def per_device(
    state_field,
    adjacency,
    edge_flips,
    conv_first,
    bias_first,
    conv_second,
    bias_second,
    norm_gain,
    up_weight,
    up_bias,
    down_weight,
    down_bias,
):
    block = state_field[0]
    first_sum = convolve(block, conv_first, adjacency, edge_flips)
    first_act = gelu_exact(first_sum + bias_first).astype(jnp.bfloat16)
    second_sum = convolve(first_act, conv_second, adjacency, edge_flips) + bias_second
    mixed = mixer(second_sum, block, norm_gain, up_weight, up_bias, down_weight, down_bias)
    return mixed[None]


def solution(mesh):
    in_specs = (P("face", "row", None, None), P(), P(), P(), P(), P(), P(), P(), P(), P(), P(), P())
    out_specs = P("face", "row", None, None)
    return jax.shard_map(
        per_device, mesh=mesh, in_specs=in_specs, out_specs=out_specs, check_vma=False
    )
```

profile of v0, /device:TPU:0, one launch (start us, length us, event | category | flops | bytes accessed | tf_op | source)
XLA Modules:
  0.0 245.8 jit_solution(8868313482546756944)
XLA Ops:
  0.0 0.9 slice_bitcast_fusion.1
  1.0 6.3 %collective-permute-start.1 = (bf16[1,256,128]{2,1,0:T(8,128)(2,1)S(1)}, bf16[1,256,128]{2,1,0:T(8,128)(2,1)S(1)}, u32[]{:S(2)}, u32[]{:S(2)}) collective-permute-start(bf16[1,256,128]{2,1,0:T(8,128)(2,1)S(1)} %get-tuple-element.59), channel_id=1, source_target_pairs={{1,0},{2,1},{3,2},{4,3},{5,4},{6,5},{7,6},{8,7},{9,8},{10,9},{11,1... | collective-permute-start | bytes 196616 | tf_op jit(solution)/shard_map/ppermute | solution.py:15
  7.3 0.8 copy.83
  8.1 3.7 %all-to-all-start = ((bf16[2,256,128]{2,0,1:T(2,128)(2,1)}), bf16[2,256,128]{2,0,1:T(2,128)(2,1)S(1)}, u32[]{:S(2)}, u32[]{:S(2)}) async-start(bf16[2,256,128]{2,0,1:T(2,128)(2,1)} %copy.83), calls=%async_computation | async-start | bytes 262144 | tf_op jit(solution)/shard_map/all_to_all | solution.py:86
  11.8 1.9 copy.132
  13.8 0.2 dynamic-slice_reduce_fusion
  14.6 28.2 %all_gather.18 = bf16[16,18,128]{2,1,0:T(8,128)(2,1)S(1)} all-gather(bf16[2,18,128]{2,1,0:T(8,128)(2,1)S(1)} %pad_maximum_fusion.8), channel_id=1, replica_groups=mesh['face'=8,'row'=16] {'face'}, dimensions={0}, use_global_device_ids=true | all-gather | bytes 82944 | tf_op jit(solution)/shard_map/all_gather | solution.py:90
  43.1 28.2 %all_gather.19 = bf16[16,16,128]{2,1,0:T(8,128)(2,1)S(1)} all-gather(bf16[2,16,128]{2,1,0:T(8,128)(2,1)S(1)} %pad_maximum_fusion.13), channel_id=1, replica_groups=mesh['face'=8,'row'=16] {'face'}, dimensions={0}, use_global_device_ids=true | all-gather | bytes 73728 | tf_op jit(solution)/shard_map/all_gather | solution.py:89
  71.5 25.2 %all_gather.20 = bf16[2,256,128]{2,1,0:T(8,128)(2,1)S(1)} all-gather(bf16[2,16,128]{2,1,0:T(8,128)(2,1)S(1)} %bitcast.187), channel_id=1, replica_groups=mesh['face'=8,'row'=16] {'row'}, dimensions={1}, use_global_device_ids=true | all-gather | bytes 139264 | tf_op jit(solution)/shard_map/all_gather | solution.py:93
  97.1 1.0 pad_maximum_fusion.4
  98.2 2.4 pad_maximum_fusion
  100.6 1.2 fusion.184
  101.9 0.3 copy.88
  102.1 0.3 copy.90
  102.4 0.3 copy.91
  102.7 0.3 copy.92
  103.0 0.3 copy.93
  103.3 0.3 copy.94
  103.5 0.3 copy.96
  103.8 0.3 copy.97
  104.1 0.4 copy-done.3
  104.5 0.4 fusion.99
  104.9 0.4 convolution_add_fusion.16
  105.3 0.4 convolution_add_fusion.15
  105.8 0.4 convolution_add_fusion.14
  106.2 0.8 copy-done.1
  107.0 0.4 convolution_add_fusion.13
  107.4 0.4 convolution_add_fusion.12
  107.8 0.4 convolution_add_fusion.11
  108.2 0.4 convolution_add_fusion.10
  108.7 0.4 convolution_add_fusion.9
  109.1 0.2 copy-done.12
  109.3 4.6 %fusion.15 = bf16[16,256,128]{2,1,0:T(8,128)(2,1)S(1)} fusion(f32[16,256,128]{2,1,0:T(8,128)S(1)} %bitcast.160, f32[128]{0:T(128)S(1)} %copy-done.12), kind=kLoop, calls=%fused_computation.47 | loop fusion | flops 34603008 | bytes 3146240 | tf_op jit(solution)/shard_map/convert_element_type | solution.py:128
  113.9 0.7 fusion.188
  114.6 0.7 collective-permute-start.2
  115.3 5.0 %collective-permute-start.3 = (bf16[1,256,128]{2,1,0:T(8,128)(2,1)}, bf16[1,256,128]{2,1,0:T(8,128)(2,1)S(1)}, u32[]{:S(2)}, u32[]{:S(2)}) collective-permute-start(bf16[1,256,128]{2,1,0:T(8,128)(2,1)} %get-tuple-element.55), channel_id=1, source_target_pairs={{1,0},{2,1},{3,2},{4,3},{5,4},{6,5},{7,6},{8,7},{9,8},{10,9},{11,1... | collective-permute-start | bytes 196616 | tf_op jit(solution)/shard_map/ppermute | solution.py:15
  120.3 0.9 pad_maximum_fusion.7
  121.2 0.8 copy.98
  122.0 3.5 %all-to-all-start.1 = ((bf16[2,256,128]{2,0,1:T(2,128)(2,1)}), bf16[2,256,128]{2,0,1:T(2,128)(2,1)S(1)}, u32[]{:S(2)}, u32[]{:S(2)}) async-start(bf16[2,256,128]{2,0,1:T(2,128)(2,1)} %copy.98), calls=%async_computation.1 | async-start | bytes 262144 | tf_op jit(solution)/shard_map/all_to_all | solution.py:86
  125.6 28.2 %all_gather.21 = bf16[16,18,128]{2,1,0:T(8,128)(2,1)S(1)} all-gather(bf16[2,18,128]{2,1,0:T(8,128)(2,1)S(1)} %pad_maximum_fusion.9), channel_id=1, replica_groups=mesh['face'=8,'row'=16] {'face'}, dimensions={0}, use_global_device_ids=true | all-gather | bytes 82944 | tf_op jit(solution)/shard_map/all_gather | solution.py:90
  153.8 0.8 convolution_convert_fusion
  154.6 0.7 reshape.162
  155.3 0.7 broadcast_select_fusion.2
  156.0 0.6 copy.102
  156.7 28.2 %all_gather.22 = bf16[16,16,128]{2,1,0:T(8,128)(2,1)S(1)} all-gather(bf16[2,16,128]{2,1,0:T(8,128)(2,1)S(1)} %pad_maximum_fusion.14), channel_id=1, replica_groups=mesh['face'=8,'row'=16] {'face'}, dimensions={0}, use_global_device_ids=true | all-gather | bytes 73728 | tf_op jit(solution)/shard_map/all_gather | solution.py:89
  184.9 0.8 fusion.34
  185.7 24.8 %all_gather.23 = bf16[2,256,128]{2,1,0:T(8,128)(2,1)S(1)} all-gather(bf16[2,16,128]{2,1,0:T(8,128)(2,1)S(1)} %bitcast.188), channel_id=1, replica_groups=mesh['face'=8,'row'=16] {'row'}, dimensions={1}, use_global_device_ids=true | all-gather | bytes 139264 | tf_op jit(solution)/shard_map/all_gather | solution.py:93
  210.7 0.9 slice_select_fusion.1
  211.8 0.6 pad_maximum_fusion.1
  212.4 0.7 fusion.187
  213.2 0.7 fusion.186
  213.9 0.2 copy-done.6
  214.1 0.5 fusion.89
  214.6 0.5 convolution_add_fusion.8
  215.1 0.5 convolution_add_fusion.7
  215.6 0.5 convolution_add_fusion.6
  216.3 4.8 %convolution_add_fusion.5 = f32[4096,128]{0,1:T(8,128)S(1)} fusion(f32[4096,128]{0,1:T(8,128)S(1)} %convolution_add_fusion.6, f32[4096,128]{1,0:T(8,128)S(1)} %convolution_add_fusion.9, f32[128]{0:T(128)S(1)} %copy-done.13, bf16[3,3,128,128]{3,2,1,0:T(8,128)(2,1)S(1)} %copy-done.6), kind=kOutput, calls=%fused_computation.26 | convolution fusion | flops 169345024 | bytes 6324736 | tf_op jit(solution)/shard_map/dot_general | solution.py:33
  221.1 0.5 convolution_add_fusion.4
  221.6 0.5 convolution_add_fusion.3
  222.1 0.5 convolution_add_fusion.2
  222.7 0.5 fusion.191
  223.3 0.2 multiply_reduce_fusion
  223.6 0.9 copy-done.2
  224.5 21.1 %fusion.12 = bf16[4096,128]{1,0:T(8,128)(2,1)} fusion(bf16[512,128]{1,0:T(8,128)(2,1)S(1)} %copy-done, bf16[4096,128]{1,0:T(8,128)(2,1)S(1)} %bitcast.162, bf16[128,512]{1,0:T(8,128)(2,1)S(1)} %copy-done.15, f32[512]{0:T(512)S(1)} %copy-done.16, f32[4096,128]{0,1:T(8,128)S(1)} %get-tuple-element.75, f32[128]{0:T(128)S(1)} %copy-done.17, ...), kind=kOutput, calls=%fused_computation.38 | convolution fusion | flops 1216348160 | bytes 4492288 | tf_op jit(solution)/shard_map/while/body/eval_jaxpr/dot_general | solution.py:56
  (79 shorter events, 2.5 us)
Async XLA Ops:
  0.0 223.6 %copy-start = (bf16[512,128]{1,0:T(8,128)(2,1)S(1)}, bf16[512,128]{1,0:T(8,128)(2,1)}, u32[]{:S(2)}) copy-start(bf16[512,128]{1,0:T(8,128)(2,1)} %param.22) | copy-start | bytes 393220
  0.0 13.8 %copy-start.8 = (s32[2,8,4]{1,2,0:T(4,128)S(1)}, s32[2,8,4]{1,2,0:T(4,128)}, u32[]{:S(2)}) copy-start(s32[2,8,4]{1,2,0:T(4,128)} %param.13) | copy-start | bytes 772
  0.0 14.1 %copy-start.10 = (s32[8,2]{0,1:T(2,128)S(1)}, s32[8,2]{0,1:T(2,128)}, u32[]{:S(2)}) copy-start(s32[8,2]{0,1:T(2,128)} %param.14) | copy-start | bytes 196
  0.9 13.4 %collective-permute-start = (bf16[1,256,128]{2,1,0:T(8,128)(2,1)S(1)}, bf16[1,256,128]{2,1,0:T(8,128)(2,1)S(1)}, u32[]{:S(2)}, u32[]{:S(2)}) collective-permute-start(bf16[1,256,128]{2,1,0:T(8,128)(2,1)S(1)} %get-tuple-element.58), channel_id=1, source_target_pairs={{0,1},{1,2},{2,3},{3,4},{4,5},{5,6},{6,7},{7,8},{8,9},{9,10},{10,1... | collective-permute-start | bytes 196616 | tf_op jit(solution)/shard_map/ppermute | solution.py:14
  1.0 13.4 %collective-permute-start.1 = (bf16[1,256,128]{2,1,0:T(8,128)(2,1)S(1)}, bf16[1,256,128]{2,1,0:T(8,128)(2,1)S(1)}, u32[]{:S(2)}, u32[]{:S(2)}) collective-permute-start(bf16[1,256,128]{2,1,0:T(8,128)(2,1)S(1)} %get-tuple-element.59), channel_id=1, source_target_pairs={{1,0},{2,1},{3,2},{4,3},{5,4},{6,5},{7,6},{8,7},{9,8},{10,9},{11,1... | collective-permute-start | bytes 196616 | tf_op jit(solution)/shard_map/ppermute | solution.py:15
  8.1 35.0 %all-to-all-start = ((bf16[2,256,128]{2,0,1:T(2,128)(2,1)}), bf16[2,256,128]{2,0,1:T(2,128)(2,1)S(1)}, u32[]{:S(2)}, u32[]{:S(2)}) async-start(bf16[2,256,128]{2,0,1:T(2,128)(2,1)} %copy.83), calls=%async_computation | async-start | bytes 262144 | tf_op jit(solution)/shard_map/all_to_all | solution.py:86
  14.1 83.1 %copy-start.11 = (s32[2]{0:T(128)}, s32[2]{0:T(128)S(1)}, u32[]{:S(2)}) copy-start(s32[2]{0:T(128)S(1)} %get-tuple-element.73) | copy-start | bytes 28
  14.3 28.7 %copy-start.9 = (pred[18]{0:T(512)(128)(4,1)}, pred[18]{0:T(512)(128)(4,1)S(1)}, u32[]{:S(2)}) copy-start(pred[18]{0:T(512)(128)(4,1)S(1)} %and_or_fusion) | copy-start | bytes 58
  103.5 1.0 copy-start.3
  105.8 1.2 copy-start.1
  108.7 0.7 copy-start.12
  114.6 10.9 %collective-permute-start.2 = (bf16[1,256,128]{2,1,0:T(8,128)(2,1)}, bf16[1,256,128]{2,1,0:T(8,128)(2,1)S(1)}, u32[]{:S(2)}, u32[]{:S(2)}) collective-permute-start(bf16[1,256,128]{2,1,0:T(8,128)(2,1)} %get-tuple-element.54), channel_id=1, source_target_pairs={{0,1},{1,2},{2,3},{3,4},{4,5},{5,6},{6,7},{7,8},{8,9},{9,10},{10,1... | collective-permute-start | bytes 196616 | tf_op jit(solution)/shard_map/ppermute | solution.py:14
  115.3 10.2 %collective-permute-start.3 = (bf16[1,256,128]{2,1,0:T(8,128)(2,1)}, bf16[1,256,128]{2,1,0:T(8,128)(2,1)S(1)}, u32[]{:S(2)}, u32[]{:S(2)}) collective-permute-start(bf16[1,256,128]{2,1,0:T(8,128)(2,1)} %get-tuple-element.55), channel_id=1, source_target_pairs={{1,0},{2,1},{3,2},{4,3},{5,4},{6,5},{7,6},{8,7},{9,8},{10,9},{11,1... | collective-permute-start | bytes 196616 | tf_op jit(solution)/shard_map/ppermute | solution.py:15
  122.0 34.7 %all-to-all-start.1 = ((bf16[2,256,128]{2,0,1:T(2,128)(2,1)}), bf16[2,256,128]{2,0,1:T(2,128)(2,1)S(1)}, u32[]{:S(2)}, u32[]{:S(2)}) async-start(bf16[2,256,128]{2,0,1:T(2,128)(2,1)} %copy.98), calls=%async_computation.1 | async-start | bytes 262144 | tf_op jit(solution)/shard_map/all_to_all | solution.py:86
  125.5 60.2 %copy-start.4 = (bf16[1,256,128]{2,1,0:T(8,128)(2,1)}, bf16[1,256,128]{2,1,0:T(8,128)(2,1)S(1)}, u32[]{:S(2)}) copy-start(bf16[1,256,128]{2,1,0:T(8,128)(2,1)S(1)} %collective-permute-done.2) | copy-start | bytes 196612
  125.5 60.2 %copy-start.5 = (bf16[1,256,128]{2,1,0:T(8,128)(2,1)}, bf16[1,256,128]{2,1,0:T(8,128)(2,1)S(1)}, u32[]{:S(2)}) copy-start(bf16[1,256,128]{2,1,0:T(8,128)(2,1)S(1)} %collective-permute-done.3) | copy-start | bytes 196612
  210.6 1.1 copy-start.7
  213.2 1.0 copy-start.6
  215.6 0.7 copy-start.13
  222.1 0.7 copy-start.14
  223.2 1.2 copy-start.2
  223.2 1.2 copy-start.15
  223.3 1.2 copy-start.16
  223.3 1.2 copy-start.17
  223.3 1.2 copy-start.18
where the time goes:
time: 251 us; the launch traced here: 246 us
  blocking collectives  163 us (65%)
  matrix products  35.6 us (14%)
  starting transfers between devices  19.3 us (8%)
  local copies, waits for them, and re-layouts  15.2 us (6%)
  other arithmetic  12.1 us (5%)
    all_gather x2, blocking collectives, gather_rims(): lax.all_gather(columns, 'face', axis=0, tiled=True)  56.4 us
    all_gather x2, blocking collectives, gather_rims(): lax.all_gather(own_pieces, 'face', axis=0, tiled=True)  56.3 us
    all_gather x2, blocking collectives, gather_rims(): beyond_rows = lax.all_gather(edge_pieces, 'row', axis=1, tiled=True)  49.9 us
    dot_general x1, matrix products, mix_block(): jnp.dot(hidden_act, down_weight, preferred_element_type=jnp.float32)  21.1 us
    dot_general x18, matrix products, convolve_padded(): jnp.dot(window, kernel[row_step, col_step], preferred_element_type=jnp.fl...  12.4 us
    ppermute x2, starting transfers between devices, extended(): after = lax.ppermute(initial, axis, down)  11.3 us
    all_to_all x2, starting transfers between devices, gather_rims(): lax.all_to_all(end_rows, 'row', split_axis=1, concat_axis=0, tiled=True)  7.26 us
  transfers between devices with their start and end apart: 6, of which 0 were waited for; matrix products, arithmetic and copies ran while one was open for 3% of the time, Pallas kernels for 0%

commit v1 on v0

v1 whole, which is shorter than its diff:
```python
import jax
import jax.numpy as jnp
from jax import lax
from jax.experimental import pallas as pl
from jax.experimental.pallas import tpu as pltpu
from jax.sharding import PartitionSpec as P

MESH = pl.DeviceIdType.MESH
bf16 = jnp.bfloat16
f32 = jnp.float32

NF = 8
NR = 16
R = 16
C = 256
CH = 128
K3 = 3 * CH
NH = 2 * NF
PIECE = C // NH
STRIP = 32
SOUT = 24


def dot(a, b):
    return jnp.dot(a, b, preferred_element_type=f32)


def gelu(v):
    return (0.5 * v) * (1.0 + lax.erf(v * 0.7071067811865476))


def put3(ref, row, v):
    zero = jnp.zeros((1, CH), bf16)
    ref[row, :, 0:CH] = jnp.concatenate([zero, v[:-1]], 0)
    ref[row, :, CH : 2 * CH] = v
    ref[row, :, 2 * CH : K3] = jnp.concatenate([v[1:], zero], 0)


def pick_row(tile, index):
    rows = lax.broadcasted_iota(jnp.int32, tile.shape, 0)
    return jnp.sum(jnp.where(rows == index, tile, 0.0), 0, keepdims=True)


def pair_weights(ref, w):
    zero = jnp.zeros((K3, CH), bf16)
    ref[0 : 3 * K3, 0:CH] = w
    ref[3 * K3 : 4 * K3, 0:CH] = zero
    ref[K3 : 4 * K3, CH : 2 * CH] = w
    ref[0:K3, CH : 2 * CH] = zero


def kernel(
    adj, flips, x, w1, b1, w2, b2, gain, wu, bu, wd, bd,
    out,
    X3, F3, T3, wp1, wp2, COL, HIN, PB, CBT, ST, SEL, SIN, EXT, XC, FS,
    colS, colR, rowS, rowR, pbS, pbR, cbS, cbR, stS, stR, selS, selR,
):
    f = lax.axis_index("face")
    r = lax.axis_index("row")
    top = r == 0
    bottom = r == NR - 1
    hot = jnp.logical_or(top, bottom)
    re = jnp.where(bottom, 1, 0)
    h = 2 * f + re

    def hot_device(m):
        return {"face": m // 2, "row": (m % 2) * (NR - 1)}

    barrier = pltpu.get_barrier_semaphore()

    def greet(device):
        pl.semaphore_signal(barrier, inc=1, device_id=device, device_id_type=MESH)

    @pl.loop(1, NF)
    def _(o):
        greet({"face": (f + o) % NF, "row": r})

    @pl.when(r > 0)
    def _():
        greet({"face": f, "row": r - 1})

    @pl.when(r < NR - 1)
    def _():
        greet({"face": f, "row": r + 1})

    @pl.when(hot)
    def _():
        @pl.loop(0, NF)
        def _(o):
            greet({"face": o, "row": (1 - re) * (NR - 1)})

    def column(c):
        base = (c // 16) * 16
        rows = [x[0, i, base : base + 16, :].astype(f32)[c - base : c - base + 1] for i in range(R)]
        return jnp.concatenate(rows, 0)

    own = [column(c) for c in (0, 1, C - 2, C - 1)]
    for k in range(4):
        COL[f, k] = own[k].astype(bf16)
        XC[k] = jnp.zeros((STRIP, CH), f32)
        XC[k, 2 : 2 + R, :] = own[k]

    @pl.when(hot)
    def _():
        firsts = jnp.concatenate([own[k][0:2] for k in range(4)] + [jnp.zeros((8, CH), f32)], 0)
        lasts = jnp.concatenate([own[k][R - 2 : R] for k in range(4)] + [jnp.zeros((8, CH), f32)], 0)
        CBT[h] = jnp.where(bottom, lasts, firsts).astype(bf16)
        PB[h] = x[0, pl.ds(re * (R - 2), 2), pl.ds(pl.multiple_of(h * PIECE, PIECE), PIECE), :]

    @pl.when(hot)
    def _():
        pl.semaphore_wait(barrier, 2 * NF)

    @pl.when(jnp.logical_not(hot))
    def _():
        pl.semaphore_wait(barrier, NF + 1)

    def col_copy(o, slot):
        return pltpu.make_async_remote_copy(
            src_ref=COL.at[slot], dst_ref=COL.at[slot],
            send_sem=colS.at[o], recv_sem=colR.at[slot],
            device_id={"face": (f + o) % NF, "row": r}, device_id_type=MESH,
        )

    def row_copy(d):
        return pltpu.make_async_remote_copy(
            src_ref=x.at[0, pl.ds((1 - d) * (R - 2), 2)], dst_ref=HIN.at[d],
            send_sem=rowS.at[d], recv_sem=rowR.at[d],
            device_id={"face": f, "row": r + 1 - 2 * d}, device_id_type=MESH,
        )

    def piece_copy(m, slot):
        return pltpu.make_async_remote_copy(
            src_ref=x.at[0, pl.ds(re * (R - 2), 2), pl.ds(pl.multiple_of(m * PIECE, PIECE), PIECE)],
            dst_ref=PB.at[slot],
            send_sem=pbS.at[m], recv_sem=pbR.at[slot],
            device_id=hot_device(m), device_id_type=MESH,
        )

    def corner_copy(m, slot):
        return pltpu.make_async_remote_copy(
            src_ref=CBT.at[slot], dst_ref=CBT.at[slot],
            send_sem=cbS.at[m], recv_sem=cbR.at[slot],
            device_id=hot_device(m), device_id_type=MESH,
        )

    @pl.when(hot)
    def _():
        @pl.loop(1, NH)
        def _(o):
            m = (h + o) % NH
            piece_copy(m, h).start()
            corner_copy(m, h).start()

    @pl.loop(1, NF)
    def _(o):
        col_copy(o, f).start()

    @pl.when(r < NR - 1)
    def _():
        row_copy(0).start()

    @pl.when(r > 0)
    def _():
        row_copy(1).start()

    pair_weights(wp1, w1[...])
    pair_weights(wp2, w2[...])
    bias1 = b1[...]
    bias2 = b2[...]
    norm_gain = gain[...]
    bias_up = bu[...]
    bias_down = bd[...]

    @pl.loop(0, R)
    def _(i):
        put3(X3, i + 2, x[0, i])

    def conv1_pairs(k, count):
        lhs = jnp.concatenate(
            [jnp.concatenate([X3[k + 2 * q + t] for t in range(4)], 1) for q in range(count)], 0
        )
        y = dot(lhs, wp1[...])
        for q in range(count):
            for j in range(2):
                v = y[C * q : C * (q + 1), CH * j : CH * (j + 1)]
                put3(F3, k + 2 * q + j, gelu(v + bias1).astype(bf16))

    @pl.loop(0, 3)
    def _(g):
        conv1_pairs(2 + 4 * g, 2)

    conv1_pairs(14, 1)

    @pl.loop(1, NF)
    def _(o):
        col_copy(o, (f + NF - o) % NF).wait_recv()

    fl, el = adj[0, f, 2], adj[1, f, 2] % 2
    fr, er = adj[0, f, 3], adj[1, f, 3] % 2
    SEL[0] = COL[fl, 3 * el]
    SEL[1] = COL[fl, 1 + el]
    SEL[2] = COL[fr, 3 * er]
    SEL[3] = COL[fr, 1 + er]

    def sel_copy(d):
        return pltpu.make_async_remote_copy(
            src_ref=SEL, dst_ref=SIN.at[d],
            send_sem=selS.at[d], recv_sem=selR.at[d],
            device_id={"face": f, "row": r + 1 - 2 * d}, device_id_type=MESH,
        )

    def chosen_copy(m, slot):
        return pltpu.make_async_remote_copy(
            src_ref=ST.at[m],
            dst_ref=HIN.at[m % 2, pl.ds(0, 2), pl.ds(pl.multiple_of(slot * PIECE, PIECE), PIECE)],
            send_sem=stS.at[m], recv_sem=stR.at[slot],
            device_id=hot_device(m), device_id_type=MESH,
        )

    @pl.when(r < NR - 1)
    def _():
        sel_copy(0).start()

    @pl.when(r > 0)
    def _():
        sel_copy(1).start()

    @pl.when(hot)
    def _():
        @pl.loop(1, NH)
        def _(o):
            piece_copy((h + o) % NH, (h + NH - o) % NH).wait_recv()

        @pl.loop(1, NH)
        def _(o):
            m = (h + o) % NH
            ST[m] = PB[2 * adj[0, m // 2, m % 2] + adj[1, m // 2, m % 2]]
            chosen_copy(m, h).start()

        HIN[re, :, pl.ds(pl.multiple_of(h * PIECE, PIECE), PIECE), :] = PB[
            2 * adj[0, f, re] + adj[1, f, re]
        ]

        @pl.loop(1, NH)
        def _(o):
            corner_copy((h + o) % NH, (h + NH - o) % NH).wait_recv()

    def mix(second, skip):
        second = second - jnp.mean(second, -1, keepdims=True)
        spread = jnp.mean(second * second, -1, keepdims=True)
        normed = (second * lax.rsqrt(spread + 1e-6) * norm_gain).astype(bf16)
        hidden = gelu(dot(normed, wu[...]) + bias_up).astype(bf16)
        return (skip.astype(f32) + (dot(hidden, wd[...]) + bias_down)).astype(bf16)

    @pl.loop(0, 3)
    def _(g):
        lhs = jnp.concatenate(
            [
                jnp.concatenate([F3[2 + 4 * g + 2 * q + t, 16 : C - 16, :] for t in range(4)], 1)
                for q in range(2)
            ],
            0,
        )
        y = dot(lhs, wp2[...])
        n = C - 32
        for q in range(2):
            for j in range(2):
                row = 2 + 4 * g + 2 * q + j
                second = y[n * q : n * (q + 1), CH * j : CH * (j + 1)] + bias2
                out[0, row, 16 : C - 16, :] = mix(second, x[0, row, 16 : C - 16, :])

    @pl.when(r > 0)
    def _():
        sel_copy(0).wait_recv()

    @pl.when(r < NR - 1)
    def _():
        sel_copy(1).wait_recv()

    @pl.when(r > 0)
    def _():
        row_copy(0).wait_recv()

    @pl.when(r < NR - 1)
    def _():
        row_copy(1).wait_recv()

    @pl.when(hot)
    def _():
        @pl.loop(1, NH)
        def _(o):
            chosen_copy((h + o) % NH, (h + NH - o) % NH).wait_recv()

    for k in range(4):
        EXT[k] = jnp.zeros((STRIP, CH), f32)
        EXT[k, 2 : 2 + R, :] = SEL[k].astype(f32)

    @pl.when(r > 0)
    def _():
        for k in range(4):
            EXT[k, 0:2, :] = SIN[0, k].astype(f32)[R - 2 : R]
        for j in range(2):
            XC[0, j : j + 1, :] = HIN[0, j, 0:16, :].astype(f32)[0:1]
            XC[3, j : j + 1, :] = HIN[0, j, C - 16 : C, :].astype(f32)[15:16]
            put3(X3, j, HIN[0, j])

    @pl.when(r < NR - 1)
    def _():
        for k in range(4):
            EXT[k, R + 2 : R + 4, :] = SIN[1, k].astype(f32)[0:2]
        for j in range(2):
            XC[0, R + 2 + j : R + 3 + j, :] = HIN[1, j, 0:16, :].astype(f32)[0:1]
            XC[3, R + 2 + j : R + 3 + j, :] = HIN[1, j, C - 16 : C, :].astype(f32)[15:16]
            put3(X3, R + 2 + j, HIN[1, j])

    def patch(ref, row, first, lanes, value, at):
        cells = ref[row, first : first + 16, lanes * CH : (lanes + 1) * CH].astype(f32)
        rows = lax.broadcasted_iota(jnp.int32, (16, CH), 0)
        ref[row, first : first + 16, lanes * CH : (lanes + 1) * CH] = jnp.where(
            rows == at, value, cells
        ).astype(bf16)

    def across(s):
        fu, eu = adj[0, f, s], adj[1, f, s]
        flip = flips[f, s]
        rows = lax.broadcasted_iota(jnp.int32, (C, C), 0)
        cols = lax.broadcasted_iota(jnp.int32, (C, C), 1)
        order = jnp.where(cols == jnp.where(flip == 1, C - 1 - rows, rows), 1.0, 0.0).astype(bf16)
        near = HIN[s, 0].astype(f32), HIN[s, 1].astype(f32)
        edge = jnp.where(eu == 1, near[1], near[0]).astype(bf16)
        turned = dot(order, jnp.concatenate([x[0, (R - 1) * s], edge], 1))
        mine = turned[:, 0:CH]
        put3(X3, 1 + (R + 1) * s, turned[:, CH : 2 * CH].astype(bf16))
        for t, v in enumerate(
            (
                jnp.where(eu == 1, near[0], mine),
                jnp.where(eu == 1, near[1], near[0]),
                jnp.where(eu == 1, mine, near[1]),
            )
        ):
            put3(T3, t, v.astype(bf16))
        for e in range(2):
            g, ge = adj[0, fu, 2 + e], adj[1, fu, 2 + e] % 2
            corner = CBT[2 * g + eu].astype(f32)
            cells = [pick_row(corner, 6 * ge + j) for j in range(2)]
            none = jnp.zeros((1, CH), f32)
            rim = (
                jnp.where(eu == 1, cells[0], none),
                jnp.where(eu == 1, cells[1], cells[0]),
                jnp.where(eu == 1, none, cells[1]),
            )
            for t in range(3):
                patch(T3, t, (C - 16) * e, 2 * e, rim[t], 15 * e)
        lhs = jnp.concatenate(
            [
                jnp.concatenate([T3[t] for t in range(3)], 1),
                jnp.concatenate([X3[1 + (R - 1) * s + t] for t in range(3)], 1),
            ],
            0,
        )
        y = gelu(dot(lhs, w1[...]) + bias1).astype(bf16)
        put3(F3, (R + 1) * s, dot(order, y[0:C]).astype(bf16))
        put3(F3, 1 + (R - 1) * s, y[C : 2 * C])

    @pl.loop(0, R + 4)
    def _(k):
        patch(X3, k, 0, 0, EXT[0, pl.ds(k, 1), :], 0)
        patch(X3, k, C - 16, 2, EXT[2, pl.ds(k, 1), :], 15)

    for s in range(2):
        is_end = (top, bottom)[s]

        @pl.when(jnp.logical_not(is_end))
        def _():
            conv1_pairs(R * s, 1)

        @pl.when(is_end)
        def _():
            across(s)
            for e in range(2):
                g0, e0 = adj[0, f, 2 + e], adj[1, f, 2 + e] % 2
                g, ge, turn = adj[0, g0, s], adj[1, g0, s], flips[g0, s]
                corner = CBT[2 * g + ge].astype(f32)
                for depth in range(2):
                    at = 3 * e0 if depth == 0 else 1 + e0
                    at = jnp.where(turn == 1, 3 - at, at)
                    EXT[2 * e + depth, 1 + (R + 1) * s : 2 + (R + 1) * s, :] = pick_row(
                        corner, 2 * at + ge
                    )

    def taps(columns):
        return jnp.concatenate(
            [v[a : a + SOUT] for a in range(3) for v in columns], 1
        ).astype(bf16)

    l0, l1, r0, r1 = EXT[0], EXT[1], EXT[2], EXT[3]
    x0, x1, x2, x3 = XC[0], XC[1], XC[2], XC[3]
    lhs = jnp.concatenate(
        [
            taps((jnp.where(el == 1, l1, x0), l0, jnp.where(el == 1, x0, l1))),
            taps((l0, x0, x1)),
            taps((x2, x3, r0)),
            taps((jnp.where(er == 1, r1, x3), r0, jnp.where(er == 1, x3, r1))),
        ],
        0,
    )
    strips = gelu(dot(lhs, w1[...]) + bias1)
    for k in range(4):
        FS[k] = strips[SOUT * k : SOUT * (k + 1)]

    for s in range(2):

        @pl.when((top, bottom)[s])
        def _():
            for k in (0, 3):
                FS[k, (R + 1) * s : (R + 1) * s + 1, :] = jnp.zeros((1, CH), f32)

    @pl.loop(0, R + 2)
    def _(k):
        patch(F3, k, 0, 0, FS[0, pl.ds(k, 1), :], 0)
        patch(F3, k, C - 16, 2, FS[3, pl.ds(k, 1), :], 15)

    @pl.loop(2, R)
    def _(k):
        v = FS[1, pl.ds(k, 1), :]
        patch(F3, k, 0, 1, v, 0)
        patch(F3, k, 0, 0, v, 1)
        v = FS[2, pl.ds(k, 1), :]
        patch(F3, k, C - 16, 1, v, 15)
        patch(F3, k, C - 16, 2, v, 14)

    @pl.loop(0, 2)
    def _(s):
        k = (R - 2) * s
        y = dot(jnp.concatenate([F3[k + t] for t in range(4)], 1), wp2[...])
        for j in range(2):
            second = y[:, CH * j : CH * (j + 1)] + bias2
            out[0, k + j] = mix(second, x[0, k + j])

    places = [(2 + 2 * q, 16 * (C // 16 - 1) * e) for q in range(R // 2 - 2) for e in range(2)]
    lhs = jnp.concatenate(
        [
            jnp.concatenate([F3[k + t, c : c + 16, :] for t in range(4)], 1)
            for k, c in places
        ],
        0,
    )
    y = dot(lhs, wp2[...])
    for j in range(2):
        skip = jnp.concatenate([x[0, k + j, c : c + 16, :] for k, c in places], 0)
        mixed = mix(y[:, CH * j : CH * (j + 1)] + bias2, skip)
        for i, (k, c) in enumerate(places):
            out[0, k + j, c : c + 16, :] = mixed[16 * i : 16 * (i + 1)]

    @pl.loop(1, NF)
    def _(o):
        col_copy(o, f).wait_send()

    @pl.when(r < NR - 1)
    def _():
        row_copy(0).wait_send()
        sel_copy(0).wait_send()

    @pl.when(r > 0)
    def _():
        row_copy(1).wait_send()
        sel_copy(1).wait_send()

    @pl.when(hot)
    def _():
        @pl.loop(1, NH)
        def _(o):
            m = (h + o) % NH
            piece_copy(m, h).wait_send()
            corner_copy(m, h).wait_send()
            chosen_copy(m, h).wait_send()


def per_device(
    state_field, adjacency, edge_flips, conv_first, bias_first, conv_second, bias_second,
    norm_gain, up_weight, up_bias, down_weight, down_bias,
):
    vmem = pl.BlockSpec(memory_space=pltpu.VMEM)
    smem = pl.BlockSpec(memory_space=pltpu.SMEM)
    dma = pltpu.SemaphoreType.DMA
    return pl.pallas_call(
        kernel,
        out_shape=jax.ShapeDtypeStruct((1, R, C, CH), bf16),
        in_specs=[smem, smem] + [vmem] * 10,
        out_specs=vmem,
        scratch_shapes=[
            pltpu.VMEM((R + 4, C, K3), bf16),
            pltpu.VMEM((R + 2, C, K3), bf16),
            pltpu.VMEM((3, C, K3), bf16),
            pltpu.VMEM((4 * K3, 2 * CH), bf16),
            pltpu.VMEM((4 * K3, 2 * CH), bf16),
            pltpu.VMEM((NF, 4, R, CH), bf16),
            pltpu.VMEM((2, 2, C, CH), bf16),
            pltpu.VMEM((NH, 2, PIECE, CH), bf16),
            pltpu.VMEM((NH, 16, CH), bf16),
            pltpu.VMEM((NH, 2, PIECE, CH), bf16),
            pltpu.VMEM((4, R, CH), bf16),
            pltpu.VMEM((2, 4, R, CH), bf16),
            pltpu.VMEM((4, STRIP, CH), f32),
            pltpu.VMEM((4, STRIP, CH), f32),
            pltpu.VMEM((4, SOUT, CH), f32),
            dma((NF,)), dma((NF,)), dma((2,)), dma((2,)),
            dma((NH,)), dma((NH,)), dma((NH,)), dma((NH,)), dma((NH,)), dma((NH,)),
            dma((2,)), dma((2,)),
        ],
        compiler_params=pltpu.CompilerParams(
            collective_id=0, has_side_effects=True, vmem_limit_bytes=56 << 20
        ),
        cost_estimate=pl.CostEstimate(flops=3_500_000_000, bytes_accessed=3_000_000, transcendentals=2_600_000),
    )(
        adjacency, edge_flips, state_field,
        conv_first.reshape(9 * CH, CH), bias_first.reshape(1, CH),
        conv_second.reshape(9 * CH, CH), bias_second.reshape(1, CH),
        norm_gain.reshape(1, CH), up_weight, up_bias.reshape(1, -1),
        down_weight, down_bias.reshape(1, CH),
    )


def solution(mesh):
    in_specs = (P("face", "row", None, None), P(), P(), P(), P(), P(), P(), P(), P(), P(), P(), P())
    out_specs = P("face", "row", None, None)
    return jax.shard_map(
        per_device, mesh=mesh, in_specs=in_specs, out_specs=out_specs, check_vma=False
    )
```

time: 251 us -> 34.5 us (0.14); the launches traced: 246 us -> 34.3 us
  blocking collectives: 163 us -> 0 us
  matrix products: 35.6 us -> 0 us
  Pallas kernels: 0 us -> 30 us
  starting transfers between devices: 19.3 us -> 0 us
  other arithmetic: 12.1 us -> 0 us
  local copies, waits for them, and re-layouts: 15.2 us -> 4.33 us
    all_gather x6 -> x0, blocking collectives: 163 us -> none  [the longest x2 56.4 us: gather_rims(): lax.all_gather(columns, 'face', axis=0, tiled=True)]
    dot_general x23 -> x0, matrix products: 35.6 us -> none  [the longest x1 21.1 us: mix_block(): jnp.dot(hidden_act, down_weight, preferred_element_type=jnp.float32)]
    pallas_call x0 -> x1, Pallas kernels: none -> 30 us  [per_device(): pl.pallas_call(kernel, out_shape=jax.ShapeDtypeStruct((1, R, C, CH), bf16...]
    ppermute x4 -> x0, starting transfers between devices: 12.1 us -> none  [the longest x2 11.3 us: extended(): after = lax.ppermute(initial, axis, down)]
    all_to_all x2 -> x0, starting transfers between devices: 7.26 us -> none  [gather_rims(): lax.all_to_all(end_rows, 'row', split_axis=1, concat_axis=0, tiled=True)]
    slice x15 -> x0, local copies, waits for them, and re-layouts: 6.46 us -> none  [the longest x11 4.88 us: convolve_padded(): padded[row_step:row_step + row_count, col_step:col_step + col_count]]
    convert_element_type x1 -> x0, other arithmetic: 4.56 us -> none  [per_device(): first_act = gelu_exact(first_sum + bias_first).astype(jnp.bfloat16)]
    concatenate x4 -> x0, other arithmetic: 4.24 us -> none  [the longest x2 3.06 us: convolve(): jnp.concatenate([side_cols[0][:, None], middle, side_cols[1][:, None]], 1)]
  transfers between devices with their start and end apart: 6 -> 0, of which waited for: 0 -> 0; matrix products, arithmetic and copies ran while one was open for 3% -> 0% of each run, Pallas kernels for 0% -> 0%
where the time goes in v1:
time: 34.5 us; the launch traced here: 34.3 us
  Pallas kernels  30 us (87%)
  local copies, waits for them, and re-layouts  4.33 us (13%)
    pallas_call x1, Pallas kernels, per_device(): pl.pallas_call(kernel, out_shape=jax.ShapeDtypeStruct((1, R, C, CH), bf16...  30 us
    unnamed x7, local copies, waits for them, and re-layouts  4.33 us

profile of v1, /device:TPU:0, one launch (start us, length us, event | category | flops | bytes accessed | tf_op | source)
XLA Modules:
  0.0 34.3 jit_solution(9915533300665471257)
XLA Ops:
  0.0 0.0 copy-start.1
  0.0 0.0 copy-start
  0.0 0.7 %copy-done.1 = s32[8,2]{0,1:T(2,128)S(1)} copy-done((s32[8,2]{0,1:T(2,128)S(1)}, s32[8,2]{0,1:T(2,128)}, u32[]{:S(2)}) %copy-start.1) | copy-done | bytes 88
  0.7 0.7 %copy.14.flips = s32[8,2]{1,0:T(8,128)} copy(s32[8,2]{0,1:T(2,128)S(1)} %copy-done.1) | data formatting | bytes 128 | tf_op args[2]
  1.3 0.0 copy-done
  1.3 0.7 %copy.13.adj = s32[2,8,4]{2,1,0:T(8,128)} copy(s32[2,8,4]{1,2,0:T(4,128)S(1)} %copy-done) | data formatting | bytes 512 | tf_op args[1]
  2.0 30.0 %shard_map.118 = bf16[1,16,256,128]{3,2,1,0:T(8,128)(2,1)} custom-call(s32[2,8,4]{2,1,0:T(8,128)} %copy.13.adj, s32[8,2]{1,0:T(8,128)} %copy.14.flips, bf16[1,16,256,128]{3,2,1,0:T(8,128)(2,1)} %x.1, bf16[1152,128]{1,0:T(8,128)(2,1)} %bitcast.7, f32[1,128]{1,0:T(1,128)} %bitcast.10, bf16[1152,128]{1,0:T(8,128)(2,1)} %bitcast.8, f32[1,128]{1,0:T(1,128)} %bitcast.11, ...), custom_call_target="tpu_custom_call" | custom-call | flops 3500000000 | bytes 3000000 | tf_op jit(solution)/shard_map/pallas_call | solution.py:487
  32.0 2.3 %copy.16 = bf16[1,16,256,128]{3,2,1,0:T(8,128)(2,1)} copy(bf16[1,16,256,128]{3,2,1,0:T(8,128)(2,1)} %shard_map.118) | data formatting | bytes 2097152
Async XLA Ops:
  0.0 0.7 %copy-start.1 = (s32[8,2]{0,1:T(2,128)S(1)}, s32[8,2]{0,1:T(2,128)}, u32[]{:S(2)}) copy-start(s32[8,2]{0,1:T(2,128)} %param.14) | copy-start | bytes 196
  0.0 1.3 %copy-start = (s32[2,8,4]{1,2,0:T(4,128)S(1)}, s32[2,8,4]{1,2,0:T(4,128)}, u32[]{:S(2)}) copy-start(s32[2,8,4]{1,2,0:T(4,128)} %param.13) | copy-start | bytes 772

commit v2 on v1

v2 whole, which is shorter than its diff:
```python
import jax
import jax.numpy as jnp
from jax import lax
from jax.experimental import pallas as pl
from jax.experimental.pallas import tpu as pltpu
from jax.sharding import PartitionSpec as P

MESH = pl.DeviceIdType.MESH
bf16 = jnp.bfloat16
f32 = jnp.float32

NF = 8
NR = 16
R = 16
C = 256
CH = 128
K3 = 3 * CH
NH = 2 * NF
PIECE = C // NF
STRIP = 32
SOUT = 24


def dot(a, b):
    return jnp.dot(a, b, preferred_element_type=f32)


def gelu(v):
    return (0.5 * v) * (1.0 + lax.erf(v * 0.7071067811865476))


def put3(ref, row, v):
    zero = jnp.zeros((1, CH), bf16)
    ref[row, :, 0:CH] = jnp.concatenate([zero, v[:-1]], 0)
    ref[row, :, CH : 2 * CH] = v
    ref[row, :, 2 * CH : K3] = jnp.concatenate([v[1:], zero], 0)


def kernel(
    adj, flips, x_hbm, w1_hbm, b1, w2_hbm, b2, gain, wu_hbm, bu, wd_hbm, bd,
    out,
    x, wp1, wp2, wu, wd, X3, F3, T3, COL, HIN, PB, CT, CTB, ST, SEL, SIN, EXT, XC, FS,
    locS, colS, colR, rowS, rowR, pbS, pbR, ctS, ctR, stS, stR, selS, selR,
):
    f = lax.axis_index("face")
    r = lax.axis_index("row")
    top = r == 0
    bottom = r == NR - 1
    hot = jnp.logical_or(top, bottom)
    middle = r == 1
    re = jnp.where(bottom, 1, 0)
    h = 2 * f + re
    place = f % 4

    def hot_device(m):
        return {"face": m // 2, "row": (m % 2) * (NR - 1)}

    local = [
        pltpu.make_async_copy(src, dst, locS.at[i])
        for i, (src, dst) in enumerate(
            (
                (x_hbm.at[0], x),
                (w1_hbm, wp1.at[pl.ds(0, 3 * K3), pl.ds(0, CH)]),
                (w1_hbm, wp1.at[pl.ds(K3, 3 * K3), pl.ds(CH, CH)]),
                (w2_hbm, wp2.at[pl.ds(0, 3 * K3), pl.ds(0, CH)]),
                (w2_hbm, wp2.at[pl.ds(K3, 3 * K3), pl.ds(CH, CH)]),
                (wu_hbm, wu),
                (wd_hbm, wd),
            )
        )
    ]
    for copy in local:
        copy.start()

    barrier = pltpu.get_barrier_semaphore()

    def greet(device):
        pl.semaphore_signal(barrier, inc=1, device_id=device, device_id_type=MESH)

    @pl.when(middle)
    def _():
        @pl.loop(0, NF)
        def _(o):
            greet({"face": o, "row": NR - 1})

        @pl.loop(0, NF)
        def _(o):
            greet({"face": o, "row": 0})

    @pl.loop(1, NF)
    def _(o):
        greet({"face": (f + o) % NF, "row": r})

    @pl.when(r > 0)
    def _():
        greet({"face": f, "row": r - 1})

    @pl.when(r < NR - 1)
    def _():
        greet({"face": f, "row": r + 1})

    def col_copy(o, slot):
        return pltpu.make_async_remote_copy(
            src_ref=COL.at[slot], dst_ref=COL.at[slot],
            send_sem=colS.at[o], recv_sem=colR.at[slot],
            device_id={"face": (f + o) % NF, "row": r}, device_id_type=MESH,
        )

    def row_copy(d):
        return pltpu.make_async_remote_copy(
            src_ref=x_hbm.at[0, pl.ds((1 - d) * (R - 2), 2)], dst_ref=HIN.at[d],
            send_sem=rowS.at[d], recv_sem=rowR.at[d],
            device_id={"face": f, "row": r + 1 - 2 * d}, device_id_type=MESH,
        )

    def piece_copy(m, slot):
        return pltpu.make_async_remote_copy(
            src_ref=x_hbm.at[
                0, pl.ds(re * (R - 2), 2), pl.ds(pl.multiple_of(m * PIECE, PIECE), PIECE)
            ],
            dst_ref=PB.at[slot],
            send_sem=pbS.at[m], recv_sem=pbR.at[slot],
            device_id={"face": m, "row": 1}, device_id_type=MESH,
        )

    def send_first():
        @pl.when(hot)
        def _():
            pl.semaphore_wait(barrier, 2 * NF)

            @pl.loop(0, NF)
            def _(o):
                piece_copy((f + o) % NF, h).start()

        @pl.when(jnp.logical_not(hot))
        def _():
            pl.semaphore_wait(barrier, NF + 1)

        @pl.loop(1, NF)
        def _(o):
            col_copy(o, f).start()

        @pl.when(r < NR - 1)
        def _():
            row_copy(0).start()

        @pl.when(r > 0)
        def _():
            row_copy(1).start()

    zero = jnp.zeros((K3, CH), bf16)
    for ref in (wp1, wp2):
        ref[3 * K3 : 4 * K3, 0:CH] = zero
        ref[0:K3, CH : 2 * CH] = zero
    bias1 = b1[...]
    bias2 = b2[...]
    norm_gain = gain[...]
    bias_up = bu[...]
    bias_down = bd[...]
    local[0].wait()

    def column(c):
        base = (c // 16) * 16
        rows = [x[i, base : base + 16, :].astype(f32)[c - base : c - base + 1] for i in range(R)]
        return jnp.concatenate(rows, 0)

    for k, c in enumerate((0, 1, C - 2, C - 1)):
        own = column(c)
        COL[f, k] = own.astype(bf16)
        XC[k] = jnp.zeros((STRIP, CH), f32)
        XC[k, 2 : 2 + R, :] = own

    @pl.when(bottom)
    def _():
        send_first()

    @pl.loop(0, R)
    def _(i):
        put3(X3, i + 2, x[i])

    def conv1_pairs(k, count):
        lhs = jnp.concatenate(
            [jnp.concatenate([X3[k + 2 * q + t] for t in range(4)], 1) for q in range(count)], 0
        )
        y = dot(lhs, wp1[...])
        for q in range(count):
            for j in range(2):
                v = y[C * q : C * (q + 1), CH * j : CH * (j + 1)]
                put3(F3, k + 2 * q + j, gelu(v + bias1).astype(bf16))

    local[1].wait()
    local[2].wait()
    conv1_pairs(14, 1)

    @pl.loop(0, 3)
    def _(g):
        @pl.when(jnp.logical_and(g == jnp.minimum(3 - place, 2), jnp.logical_not(bottom)))
        def _():
            send_first()

        conv1_pairs(2 + 4 * g, 2)

    for copy in local[3:]:
        copy.wait()

    fl, el = adj[0, 2, f], adj[1, 2, f] % 2
    fr, er = adj[0, 3, f], adj[1, 3, f] % 2

    def sel_copy(d):
        return pltpu.make_async_remote_copy(
            src_ref=SEL, dst_ref=SIN.at[d],
            send_sem=selS.at[d], recv_sem=selR.at[d],
            device_id={"face": f, "row": r + 1 - 2 * d}, device_id_type=MESH,
        )

    def send_strips():
        @pl.loop(1, NF)
        def _(o):
            col_copy(o, (f + NF - o) % NF).wait_recv()

        SEL[0] = COL[fl, 3 * el]
        SEL[1] = COL[fl, 1 + el]
        SEL[2] = COL[fr, 3 * er]
        SEL[3] = COL[fr, 1 + er]

        @pl.when(r < NR - 1)
        def _():
            sel_copy(0).start()

        @pl.when(r > 0)
        def _():
            sel_copy(1).start()

    def chosen_copy(m, slot):
        return pltpu.make_async_remote_copy(
            src_ref=ST.at[m],
            dst_ref=HIN.at[m % 2, pl.ds(0, 2), pl.ds(pl.multiple_of(slot * PIECE, PIECE), PIECE)],
            send_sem=stS.at[m], recv_sem=stR.at[slot],
            device_id=hot_device(m), device_id_type=MESH,
        )

    def corner_copy(m, side):
        return pltpu.make_async_remote_copy(
            src_ref=CT, dst_ref=CTB.at[side],
            send_sem=ctS.at[m], recv_sem=ctR.at[side],
            device_id=hot_device(m), device_id_type=MESH,
        )

    has_corner = jnp.logical_or(f == 0, f == NF - 1)
    side = jnp.where(f == 0, 0, 1)

    def order_of(o):
        return 2 * (o % NF) + o // NF

    def send_pieces():
        @pl.loop(0, NH)
        def _(m):
            pltpu.make_async_remote_copy(
                src_ref=ST.at[m], dst_ref=PB.at[m], send_sem=stS.at[m], recv_sem=pbR.at[m],
                device_id=hot_device(m), device_id_type=MESH,
            ).wait_recv()

        @pl.when(has_corner)
        def _():
            for g in range(NH // 4):
                cells = []
                for e in range(4 * g, 4 * g + 4):
                    for j in range(2):
                        first = PB[e, j, 0:16, :].astype(f32)[0:2]
                        last = PB[e, j, PIECE - 16 : PIECE, :].astype(f32)[14:16]
                        cells.append(jnp.where(f == 0, first, last))
                CT[g] = jnp.concatenate(cells, 0).astype(bf16)

        @pl.loop(0, NH)
        def _(o):
            m = order_of(o)
            ST[m] = PB[2 * adj[0, m % 2, m // 2] + adj[1, m % 2, m // 2]]
            chosen_copy(m, f).start()

            @pl.when(has_corner)
            def _():
                corner_copy(m, side).start()

    def mix(second, skip):
        second = second - jnp.mean(second, -1, keepdims=True)
        spread = jnp.mean(second * second, -1, keepdims=True)
        normed = (second * lax.rsqrt(spread + 1e-6) * norm_gain).astype(bf16)
        hidden = gelu(dot(normed, wu[...]) + bias_up).astype(bf16)
        return (skip.astype(f32) + (dot(hidden, wd[...]) + bias_down)).astype(bf16)

    @pl.loop(0, 3)
    def _(g):
        @pl.when(g == jnp.where(place == 0, 1, 0))
        def _():
            send_strips()

        @pl.when(jnp.logical_and(middle, jnp.logical_and(g == 2, place > 1)))
        def _():
            send_pieces()

        lhs = jnp.concatenate(
            [
                jnp.concatenate([F3[2 + 4 * g + 2 * q + t, 16 : C - 16, :] for t in range(4)], 1)
                for q in range(2)
            ],
            0,
        )
        y = dot(lhs, wp2[...])
        n = C - 32
        for q in range(2):
            for j in range(2):
                row = 2 + 4 * g + 2 * q + j
                second = y[n * q : n * (q + 1), CH * j : CH * (j + 1)] + bias2
                out[0, row, 16 : C - 16, :] = mix(second, x[row, 16 : C - 16, :])

    @pl.when(jnp.logical_and(middle, place <= 1))
    def _():
        send_pieces()

    @pl.when(r > 0)
    def _():
        sel_copy(0).wait_recv()
        row_copy(0).wait_recv()

    @pl.when(r < NR - 1)
    def _():
        sel_copy(1).wait_recv()
        row_copy(1).wait_recv()

    for k in range(4):
        EXT[k] = jnp.zeros((STRIP, CH), f32)
        EXT[k, 2 : 2 + R, :] = SEL[k].astype(f32)

    @pl.when(r > 0)
    def _():
        for k in range(4):
            EXT[k, 0:2, :] = SIN[0, k].astype(f32)[R - 2 : R]
        for j in range(2):
            XC[0, j : j + 1, :] = HIN[0, j, 0:16, :].astype(f32)[0:1]
            XC[3, j : j + 1, :] = HIN[0, j, C - 16 : C, :].astype(f32)[15:16]
            put3(X3, j, HIN[0, j])

    @pl.when(r < NR - 1)
    def _():
        for k in range(4):
            EXT[k, R + 2 : R + 4, :] = SIN[1, k].astype(f32)[0:2]
        for j in range(2):
            XC[0, R + 2 + j : R + 3 + j, :] = HIN[1, j, 0:16, :].astype(f32)[0:1]
            XC[3, R + 2 + j : R + 3 + j, :] = HIN[1, j, C - 16 : C, :].astype(f32)[15:16]
            put3(X3, R + 2 + j, HIN[1, j])

    def patch(ref, row, first, lanes, value, at):
        cells = ref[row, first : first + 16, lanes * CH : (lanes + 1) * CH].astype(f32)
        rows = lax.broadcasted_iota(jnp.int32, (16, CH), 0)
        ref[row, first : first + 16, lanes * CH : (lanes + 1) * CH] = jnp.where(
            rows == at, value, cells
        ).astype(bf16)

    @pl.loop(0, R + 4)
    def _(k):
        patch(X3, k, 0, 0, EXT[0, pl.ds(k, 1), :], 0)
        patch(X3, k, C - 16, 2, EXT[2, pl.ds(k, 1), :], 15)

    def taps(columns):
        return jnp.concatenate([v[a : a + v.shape[0] - 2] for a in range(3) for v in columns], 1)

    def outer_left(l0, l1, x0):
        return taps((jnp.where(el == 1, l1, x0), l0, jnp.where(el == 1, x0, l1)))

    def outer_right(r0, r1, x3):
        return taps((jnp.where(er == 1, r1, x3), r0, jnp.where(er == 1, x3, r1)))

    count = SOUT + 2
    lhs = jnp.concatenate(
        [
            outer_left(EXT[0, 0:count], EXT[1, 0:count], XC[0, 0:count]),
            taps((EXT[0, 0:count], XC[0, 0:count], XC[1, 0:count])),
            taps((XC[2, 0:count], XC[3, 0:count], EXT[2, 0:count])),
            outer_right(EXT[2, 0:count], EXT[3, 0:count], XC[3, 0:count]),
        ],
        0,
    )
    strips = gelu(dot(lhs.astype(bf16), wp1[0 : 3 * K3, 0:CH]) + bias1)
    for k in range(4):
        FS[k] = strips[SOUT * k : SOUT * (k + 1)]

    for s in range(2):

        @pl.when(jnp.logical_not((top, bottom)[s]))
        def _():
            conv1_pairs(R * s, 1)

    @pl.loop(0, R + 2)
    def _(k):
        patch(F3, k, 0, 0, FS[0, pl.ds(k, 1), :], 0)
        patch(F3, k, C - 16, 2, FS[3, pl.ds(k, 1), :], 15)

    @pl.loop(2, R)
    def _(k):
        v = FS[1, pl.ds(k, 1), :]
        patch(F3, k, 0, 1, v, 0)
        patch(F3, k, 0, 0, v, 1)
        v = FS[2, pl.ds(k, 1), :]
        patch(F3, k, C - 16, 1, v, 15)
        patch(F3, k, C - 16, 2, v, 14)

    def outer_rows(s):
        k = (R - 2) * s
        y = dot(jnp.concatenate([F3[k + t] for t in range(4)], 1), wp2[...])
        for j in range(2):
            second = y[:, CH * j : CH * (j + 1)] + bias2
            out[0, k + j] = mix(second, x[k + j])

    @pl.loop(0, 2)
    def _(s):
        @pl.when(jnp.logical_not(jnp.where(s == 0, top, bottom)))
        def _():
            outer_rows(s)

    places = [(2 + 2 * q, 16 * (C // 16 - 1) * e) for q in range(R // 2 - 2) for e in range(2)]
    lhs = jnp.concatenate(
        [
            jnp.concatenate([F3[k + t, c : c + 16, :] for t in range(4)], 1)
            for k, c in places
        ],
        0,
    )
    y = dot(lhs, wp2[...])
    for j in range(2):
        skip = jnp.concatenate([x[k + j, c : c + 16, :] for k, c in places], 0)
        mixed = mix(y[:, CH * j : CH * (j + 1)] + bias2, skip)
        for i, (k, c) in enumerate(places):
            out[0, k + j, c : c + 16, :] = mixed[16 * i : 16 * (i + 1)]

    def corner_cell(face, edge, j, at):
        e = 2 * face + edge
        tile = CTB[at // 2, e // 4].astype(f32)
        rows = lax.broadcasted_iota(jnp.int32, tile.shape, 0)
        return jnp.sum(
            jnp.where(rows == 4 * (e % 4) + 2 * j + at % 2, tile, 0.0), 0, keepdims=True
        )

    @pl.when(hot)
    def _():
        s = re

        @pl.loop(0, NF)
        def _(m):
            chosen_copy(h, m).wait_recv()

        for d in range(2):
            corner_copy(h, d).wait_recv()

        fu, eu = adj[0, s, f], adj[1, s, f]
        flip = flips[s, f]
        rows = lax.broadcasted_iota(jnp.int32, (C, C), 0)
        cols = lax.broadcasted_iota(jnp.int32, (C, C), 1)
        order = jnp.where(cols == jnp.where(flip == 1, C - 1 - rows, rows), 1.0, 0.0).astype(bf16)
        near = HIN[s, 0].astype(f32), HIN[s, 1].astype(f32)
        edge = jnp.where(eu == 1, near[1], near[0]).astype(bf16)
        turned = dot(order, jnp.concatenate([x[(R - 1) * s], edge], 1))
        mine = turned[:, 0:CH]
        put3(X3, 1 + (R + 1) * s, turned[:, CH : 2 * CH].astype(bf16))
        for t, v in enumerate(
            (
                jnp.where(eu == 1, near[0], mine),
                jnp.where(eu == 1, near[1], near[0]),
                jnp.where(eu == 1, mine, near[1]),
            )
        ):
            put3(T3, t, v.astype(bf16))
        none = jnp.zeros((1, CH), f32)
        for e in range(2):
            g, ge = adj[0, 2 + e, fu], adj[1, 2 + e, fu] % 2
            cells = [corner_cell(g, eu, j, 3 * ge) for j in range(2)]
            rim = (
                jnp.where(eu == 1, cells[0], none),
                jnp.where(eu == 1, cells[1], cells[0]),
                jnp.where(eu == 1, none, cells[1]),
            )
            for t in range(3):
                patch(T3, t, (C - 16) * e, 2 * e, rim[t], 15 * e)
            g0, e0 = adj[0, 2 + e, f], adj[1, 2 + e, f] % 2
            g, ge, turn = adj[0, s, g0], adj[1, s, g0], flips[s, g0]
            for depth in range(2):
                at = 3 * e0 if depth == 0 else 1 + e0
                at = jnp.where(turn == 1, 3 - at, at)
                EXT[2 * e + depth, pl.ds(1 + (R + 1) * s, 1), :] = corner_cell(g, ge, ge, at)

        near_rows = pl.ds(1 + (R - 1) * s, 10)
        strip = jnp.concatenate(
            [
                outer_left(EXT[0, near_rows], EXT[1, near_rows], XC[0, near_rows]),
                outer_right(EXT[2, near_rows], EXT[3, near_rows], XC[3, near_rows]),
            ],
            0,
        ).astype(bf16)
        lhs = jnp.concatenate(
            [
                jnp.concatenate([T3[t] for t in range(3)], 1),
                jnp.concatenate([X3[1 + (R - 1) * s + t] for t in range(3)], 1),
                strip,
            ],
            0,
        )
        y = gelu(dot(lhs, wp1[0 : 3 * K3, 0:CH]) + bias1)
        put3(F3, (R + 1) * s, dot(order, y[0:C].astype(bf16)).astype(bf16))
        put3(F3, 1 + (R - 1) * s, y[C : 2 * C].astype(bf16))
        patch(F3, 1 + (R - 1) * s, 0, 0, y[2 * C : 2 * C + 1], 0)
        patch(F3, 1 + (R - 1) * s, C - 16, 2, y[2 * C + 8 : 2 * C + 9], 15)
        outer_rows(s)

    @pl.loop(1, NF)
    def _(o):
        col_copy(o, f).wait_send()

    @pl.when(r < NR - 1)
    def _():
        row_copy(0).wait_send()
        sel_copy(0).wait_send()

    @pl.when(r > 0)
    def _():
        row_copy(1).wait_send()
        sel_copy(1).wait_send()

    @pl.when(hot)
    def _():
        @pl.loop(0, NF)
        def _(m):
            piece_copy(m, h).wait_send()

    @pl.when(middle)
    def _():
        @pl.loop(0, NH)
        def _(m):
            chosen_copy(m, f).wait_send()

            @pl.when(has_corner)
            def _():
                corner_copy(m, side).wait_send()


def per_device(
    state_field, adjacency, edge_flips, conv_first, bias_first, conv_second, bias_second,
    norm_gain, up_weight, up_bias, down_weight, down_bias,
):
    vmem = pl.BlockSpec(memory_space=pltpu.VMEM)
    smem = pl.BlockSpec(memory_space=pltpu.SMEM)
    hbm = pl.BlockSpec(memory_space=pl.ANY)
    dma = pltpu.SemaphoreType.DMA
    return pl.pallas_call(
        kernel,
        out_shape=jax.ShapeDtypeStruct((1, R, C, CH), bf16),
        in_specs=[smem, smem, hbm, hbm, vmem, hbm, vmem, vmem, hbm, vmem, hbm, vmem],
        out_specs=vmem,
        scratch_shapes=[
            pltpu.VMEM((R, C, CH), bf16),
            pltpu.VMEM((4 * K3, 2 * CH), bf16),
            pltpu.VMEM((4 * K3, 2 * CH), bf16),
            pltpu.VMEM(up_weight.shape, bf16),
            pltpu.VMEM(down_weight.shape, bf16),
            pltpu.VMEM((R + 4, C, K3), bf16),
            pltpu.VMEM((R + 2, C, K3), bf16),
            pltpu.VMEM((3, C, K3), bf16),
            pltpu.VMEM((NF, 4, R, CH), bf16),
            pltpu.VMEM((2, 2, C, CH), bf16),
            pltpu.VMEM((NH, 2, PIECE, CH), bf16),
            pltpu.VMEM((NH // 4, 16, CH), bf16),
            pltpu.VMEM((2, NH // 4, 16, CH), bf16),
            pltpu.VMEM((NH, 2, PIECE, CH), bf16),
            pltpu.VMEM((4, R, CH), bf16),
            pltpu.VMEM((2, 4, R, CH), bf16),
            pltpu.VMEM((4, STRIP, CH), f32),
            pltpu.VMEM((4, STRIP, CH), f32),
            pltpu.VMEM((4, SOUT, CH), f32),
            dma((7,)), dma((NF,)), dma((NF,)), dma((2,)), dma((2,)),
            dma((NF,)), dma((NH,)), dma((NH,)), dma((2,)), dma((NH,)), dma((NF,)),
            dma((2,)), dma((2,)),
        ],
        compiler_params=pltpu.CompilerParams(
            collective_id=0, has_side_effects=True, vmem_limit_bytes=56 << 20
        ),
        cost_estimate=pl.CostEstimate(
            flops=3_500_000_000, bytes_accessed=3_000_000, transcendentals=2_600_000
        ),
    )(
        jnp.transpose(adjacency, (0, 2, 1)), jnp.transpose(edge_flips), state_field,
        conv_first.reshape(9 * CH, CH), bias_first.reshape(1, CH),
        conv_second.reshape(9 * CH, CH), bias_second.reshape(1, CH),
        norm_gain.reshape(1, CH), up_weight, up_bias.reshape(1, -1),
        down_weight, down_bias.reshape(1, CH),
    )


def solution(mesh):
    in_specs = (P("face", "row", None, None), P(), P(), P(), P(), P(), P(), P(), P(), P(), P(), P())
    out_specs = P("face", "row", None, None)
    return jax.shard_map(
        per_device, mesh=mesh, in_specs=in_specs, out_specs=out_specs, check_vma=False
    )
```

time: 34.5 us -> 26.8 us (0.78)
  the two profiles are of different devices: /device:TPU:0 before, /device:TPU:6 now
where the time goes in v2:
time: 26.8 us; the launch traced here: 26.6 us
  Pallas kernels  24.3 us (91%)
  local copies, waits for them, and re-layouts  2.3 us (9%)
    pallas_call x1, Pallas kernels, per_device(): pl.pallas_call(kernel, out_shape=jax.ShapeDtypeStruct((1, R, C, CH), bf16...  24.3 us
    unnamed x1, local copies, waits for them, and re-layouts  2.3 us

profile of v2, /device:TPU:6, one launch (start us, length us, event | category | flops | bytes accessed | tf_op | source)
XLA Modules:
  0.0 26.6 jit_solution(7473396747387206629)
XLA Ops:
  0.0 24.3 %shard_map.118 = bf16[1,16,256,128]{3,2,1,0:T(8,128)(2,1)} custom-call(s32[2,4,8]{2,1,0:T(4,128)} %bitcast.11, s32[2,8]{1,0:T(2,128)} %bitcast.13, bf16[1,16,256,128]{3,2,1,0:T(8,128)(2,1)} %x_hbm.1, bf16[1152,128]{1,0:T(8,128)(2,1)} %bitcast.9, f32[1,128]{1,0:T(1,128)} %bitcast.14, bf16[1152,128]{1,0:T(8,128)(2,1)} %bitcast.10, f32[1,128]{1,0:T(1,128)} %bitcast.15, ...), custom_call_target="tpu_custom_call" | custom-call | flops 3500000000 | bytes 3000000 | tf_op jit(solution)/shard_map/pallas_call | solution.py:552
  24.3 2.3 %copy.14 = bf16[1,16,256,128]{3,2,1,0:T(8,128)(2,1)} copy(bf16[1,16,256,128]{3,2,1,0:T(8,128)(2,1)} %shard_map.118) | data formatting | bytes 2097152

commit v3 on v2

--- a/solution.py
+++ b/solution.py
@@ -39,8 +39,8 @@
 def kernel(
     adj, flips, x_hbm, w1_hbm, b1, w2_hbm, b2, gain, wu_hbm, bu, wd_hbm, bd,
     out,
-    x, wp1, wp2, wu, wd, X3, F3, T3, COL, HIN, PB, CT, CTB, ST, SEL, SIN, EXT, XC, FS,
-    locS, colS, colR, rowS, rowR, pbS, pbR, ctS, ctR, stS, stR, selS, selR,
+    x, wp1, wp2, wu, wd, X3, F3, T3, NS, P15, COL, HIN, PB, CT, CTB, ST, SEL, SIN, EXT, XC, FS,
+    locS, viaS, viaR, relS, colS, colR, rowS, rowR, pbS, pbR, ctS, ctR, stS, stR, selS, selR,
 ):
     f = lax.axis_index("face")
     r = lax.axis_index("row")
@@ -48,6 +48,7 @@
     bottom = r == NR - 1
     hot = jnp.logical_or(top, bottom)
     middle = r == 1
+    relay = r == NR - 2
     re = jnp.where(bottom, 1, 0)
     h = 2 * f + re
     place = f % 4
@@ -89,7 +90,7 @@
 
     @pl.loop(1, NF)
     def _(o):
-        greet({"face": (f + o) % NF, "row": r})
+        greet({"face": (f + o) % NF, "row": jnp.where(bottom, NR - 2, r)})
 
     @pl.when(r > 0)
     def _():
@@ -123,30 +124,61 @@
             device_id={"face": m, "row": 1}, device_id_type=MESH,
         )
 
+    def to_relay():
+        return pltpu.make_async_remote_copy(
+            src_ref=COL.at[f], dst_ref=P15, send_sem=viaS.at[0], recv_sem=viaR.at[0],
+            device_id={"face": f, "row": NR - 2}, device_id_type=MESH,
+        )
+
+    def relay_copy(o):
+        return pltpu.make_async_remote_copy(
+            src_ref=P15, dst_ref=COL.at[f], send_sem=relS.at[o], recv_sem=colR.at[f],
+            device_id={"face": (f + o) % NF, "row": NR - 1}, device_id_type=MESH,
+        )
+
+    def send_end_row():
+        @pl.loop(0, NF)
+        def _(o):
+            piece_copy((f + o) % NF, h).start()
+
     def send_first():
-        @pl.when(hot)
+        busy = jnp.logical_or(top, relay)
+
+        @pl.when(busy)
         def _():
             pl.semaphore_wait(barrier, 2 * NF)
 
-            @pl.loop(0, NF)
+        @pl.when(jnp.logical_not(busy))
+        def _():
+            pl.semaphore_wait(barrier, NF + 1)
+
+        @pl.loop(1, NF)
+        def _(o):
+            col_copy(o, f).start()
+
+        @pl.when(top)
+        def _():
+            send_end_row()
+
+        row_copy(0).start()
+
+        @pl.when(r > 0)
+        def _():
+            row_copy(1).start()
+
+        @pl.when(relay)
+        def _():
+            to_relay().wait_recv()
+
+            @pl.loop(1, NF)
             def _(o):
-                piece_copy((f + o) % NF, h).start()
-
-        @pl.when(jnp.logical_not(hot))
-        def _():
-            pl.semaphore_wait(barrier, NF + 1)
-
-        @pl.loop(1, NF)
-        def _(o):
-            col_copy(o, f).start()
-
-        @pl.when(r < NR - 1)
-        def _():
-            row_copy(0).start()
-
-        @pl.when(r > 0)
-        def _():
-            row_copy(1).start()
+                relay_copy(o).start()
+
+    @pl.when(bottom)
+    def _():
+        pl.semaphore_wait(barrier, NF + 1)
+        send_end_row()
+        row_copy(1).start()
 
     zero = jnp.zeros((K3, CH), bf16)
     for ref in (wp1, wp2):
@@ -172,36 +204,62 @@
 
     @pl.when(bottom)
     def _():
-        send_first()
+        to_relay().start()
+
+    def send_at(point):
+        @pl.when(jnp.logical_and(jnp.minimum(3 - place, 2) == point, jnp.logical_not(bottom)))
+        def _():
+            send_first()
+
+    send_at(0)
 
     @pl.loop(0, R)
     def _(i):
         put3(X3, i + 2, x[i])
 
-    def conv1_pairs(k, count):
+    def conv1_pairs(starts):
         lhs = jnp.concatenate(
-            [jnp.concatenate([X3[k + 2 * q + t] for t in range(4)], 1) for q in range(count)], 0
+            [jnp.concatenate([X3[k + t] for t in range(4)], 1) for k in starts], 0
         )
         y = dot(lhs, wp1[...])
-        for q in range(count):
+        for q, k in enumerate(starts):
             for j in range(2):
                 v = y[C * q : C * (q + 1), CH * j : CH * (j + 1)]
-                put3(F3, k + 2 * q + j, gelu(v + bias1).astype(bf16))
+                put3(F3, k + j, gelu(v + bias1).astype(bf16))
 
     local[1].wait()
     local[2].wait()
-    conv1_pairs(14, 1)
-
-    @pl.loop(0, 3)
-    def _(g):
-        @pl.when(jnp.logical_and(g == jnp.minimum(3 - place, 2), jnp.logical_not(bottom)))
-        def _():
-            send_first()
-
-        conv1_pairs(2 + 4 * g, 2)
+    conv1_pairs(range(2, R, 2))
+    send_at(1)
 
     for copy in local[3:]:
         copy.wait()
+
+    def conv2_norm(segments):
+        lhs = jnp.concatenate(
+            [jnp.concatenate([F3[k + t, a:b, :] for t in range(4)], 1) for k, a, b in segments], 0
+        )
+        y = dot(lhs, wp2[...])
+        parts, at = [], 0
+        for k, a, b in segments:
+            parts += [y[at : at + b - a, CH * j : CH * (j + 1)] for j in range(2)]
+            at += b - a
+        second = jnp.concatenate(parts, 0) + bias2
+        second = second - jnp.mean(second, -1, keepdims=True)
+        spread = jnp.mean(second * second, -1, keepdims=True)
+        return (second * lax.rsqrt(spread + 1e-6) * norm_gain).astype(bf16)
+
+    def pointwise(normed, skip):
+        hidden = gelu(dot(normed, wu[...]) + bias_up).astype(bf16)
+        return (skip.astype(f32) + (dot(hidden, wd[...]) + bias_down)).astype(bf16)
+
+    def finish(segments):
+        cells = [(k + j, a, b) for k, a, b in segments for j in range(2)]
+        skip = jnp.concatenate([x[k, a:b, :] for k, a, b in cells], 0)
+        mixed, at = pointwise(conv2_norm(segments), skip), 0
+        for k, a, b in cells:
+            out[0, k, a:b, :] = mixed[at : at + b - a]
+            at += b - a
 
     fl, el = adj[0, 2, f], adj[1, 2, f] % 2
     fr, er = adj[0, 3, f], adj[1, 3, f] % 2
@@ -281,51 +339,61 @@
             def _():
                 corner_copy(m, side).start()
 
-    def mix(second, skip):
-        second = second - jnp.mean(second, -1, keepdims=True)
-        spread = jnp.mean(second * second, -1, keepdims=True)
-        normed = (second * lax.rsqrt(spread + 1e-6) * norm_gain).astype(bf16)
-        hidden = gelu(dot(normed, wu[...]) + bias_up).astype(bf16)
-        return (skip.astype(f32) + (dot(hidden, wd[...]) + bias_down)).astype(bf16)
-
-    @pl.loop(0, 3)
+    inner = C - 32
+    normed = conv2_norm([(k, 16, C - 16) for k in range(2, R - 2, 2)])
+    for i in range(R - 4):
+        NS[i] = normed[inner * i : inner * (i + 1)]
+    send_at(2)
+
+    @pl.loop(0, 2)
     def _(g):
-        @pl.when(g == jnp.where(place == 0, 1, 0))
+        rows = [(R // 2 - 2) * g + i for i in range(R // 2 - 2)]
+        skip = jnp.concatenate([x[2 + i, 16 : C - 16, :] for i in rows], 0)
+        mixed = pointwise(jnp.concatenate([NS[i] for i in rows], 0), skip)
+        for q, i in enumerate(rows):
+            out[0, 2 + i, 16 : C - 16, :] = mixed[inner * q : inner * (q + 1)]
+
+        @pl.when(g == jnp.where(place < 2, 1, 0))
         def _():
             send_strips()
 
-        @pl.when(jnp.logical_and(middle, jnp.logical_and(g == 2, place > 1)))
-        def _():
-            send_pieces()
-
-        lhs = jnp.concatenate(
-            [
-                jnp.concatenate([F3[2 + 4 * g + 2 * q + t, 16 : C - 16, :] for t in range(4)], 1)
-                for q in range(2)
-            ],
-            0,
-        )
-        y = dot(lhs, wp2[...])
-        n = C - 32
-        for q in range(2):
-            for j in range(2):
-                row = 2 + 4 * g + 2 * q + j
-                second = y[n * q : n * (q + 1), CH * j : CH * (j + 1)] + bias2
-                out[0, row, 16 : C - 16, :] = mix(second, x[row, 16 : C - 16, :])
-
-    @pl.when(jnp.logical_and(middle, place <= 1))
+    @pl.when(jnp.logical_and(middle, place > 0))
     def _():
         send_pieces()
 
     @pl.when(r > 0)
     def _():
+        row_copy(0).wait_recv()
+        for j in range(2):
+            put3(X3, j, HIN[0, j])
+
+    @pl.when(r < NR - 1)
+    def _():
+        row_copy(1).wait_recv()
+        for j in range(2):
+            put3(X3, R + 2 + j, HIN[1, j])
+
+    @pl.when(jnp.logical_not(hot))
+    def _():
+        conv1_pairs((0, R))
+        finish([(k, 16, C - 16) for k in (0, R - 2)])
+
+    @pl.when(hot)
+    def _():
+        conv1_pairs((R * (1 - re),))
+        finish([((R - 2) * (1 - re), 16, C - 16)])
+
+    @pl.when(jnp.logical_and(middle, place == 0))
+    def _():
+        send_pieces()
+
+    @pl.when(r > 0)
+    def _():
         sel_copy(0).wait_recv()
-        row_copy(0).wait_recv()
 
     @pl.when(r < NR - 1)
     def _():
         sel_copy(1).wait_recv()
-        row_copy(1).wait_recv()
 
     for k in range(4):
         EXT[k] = jnp.zeros((STRIP, CH), f32)
@@ -336,18 +404,18 @@
         for k in range(4):
             EXT[k, 0:2, :] = SIN[0, k].astype(f32)[R - 2 : R]
         for j in range(2):
-            XC[0, j : j + 1, :] = HIN[0, j, 0:16, :].astype(f32)[0:1]
-            XC[3, j : j + 1, :] = HIN[0, j, C - 16 : C, :].astype(f32)[15:16]
-            put3(X3, j, HIN[0, j])
+            first, last = HIN[0, j, 0:16, :].astype(f32), HIN[0, j, C - 16 : C, :].astype(f32)
+            for k, v in enumerate((first[0:1], first[1:2], last[14:15], last[15:16])):
+                XC[k, j : j + 1, :] = v
 
     @pl.when(r < NR - 1)
     def _():
         for k in range(4):
             EXT[k, R + 2 : R + 4, :] = SIN[1, k].astype(f32)[0:2]
         for j in range(2):
-            XC[0, R + 2 + j : R + 3 + j, :] = HIN[1, j, 0:16, :].astype(f32)[0:1]
-            XC[3, R + 2 + j : R + 3 + j, :] = HIN[1, j, C - 16 : C, :].astype(f32)[15:16]
-            put3(X3, R + 2 + j, HIN[1, j])
+            first, last = HIN[1, j, 0:16, :].astype(f32), HIN[1, j, C - 16 : C, :].astype(f32)
+            for k, v in enumerate((first[0:1], first[1:2], last[14:15], last[15:16])):
+                XC[k, R + 2 + j : R + 3 + j, :] = v
 
     def patch(ref, row, first, lanes, value, at):
         cells = ref[row, first : first + 16, lanes * CH : (lanes + 1) * CH].astype(f32)
@@ -355,11 +423,6 @@
         ref[row, first : first + 16, lanes * CH : (lanes + 1) * CH] = jnp.where(
             rows == at, value, cells
         ).astype(bf16)
-
-    @pl.loop(0, R + 4)
-    def _(k):
-        patch(X3, k, 0, 0, EXT[0, pl.ds(k, 1), :], 0)
-        patch(X3, k, C - 16, 2, EXT[2, pl.ds(k, 1), :], 15)
 
     def taps(columns):
         return jnp.concatenate([v[a : a + v.shape[0] - 2] for a in range(3) for v in columns], 1)
@@ -384,19 +447,10 @@
     for k in range(4):
         FS[k] = strips[SOUT * k : SOUT * (k + 1)]
 
-    for s in range(2):
-
-        @pl.when(jnp.logical_not((top, bottom)[s]))
-        def _():
-            conv1_pairs(R * s, 1)
-
     @pl.loop(0, R + 2)
     def _(k):
         patch(F3, k, 0, 0, FS[0, pl.ds(k, 1), :], 0)
         patch(F3, k, C - 16, 2, FS[3, pl.ds(k, 1), :], 15)
-
-    @pl.loop(2, R)
-    def _(k):
         v = FS[1, pl.ds(k, 1), :]
         patch(F3, k, 0, 1, v, 0)
         patch(F3, k, 0, 0, v, 1)
@@ -404,33 +458,7 @@
         patch(F3, k, C - 16, 1, v, 15)
         patch(F3, k, C - 16, 2, v, 14)
 
-    def outer_rows(s):
-        k = (R - 2) * s
-        y = dot(jnp.concatenate([F3[k + t] for t in range(4)], 1), wp2[...])
-        for j in range(2):
-            second = y[:, CH * j : CH * (j + 1)] + bias2
-            out[0, k + j] = mix(second, x[k + j])
-
-    @pl.loop(0, 2)
-    def _(s):
-        @pl.when(jnp.logical_not(jnp.where(s == 0, top, bottom)))
-        def _():
-            outer_rows(s)
-
-    places = [(2 + 2 * q, 16 * (C // 16 - 1) * e) for q in range(R // 2 - 2) for e in range(2)]
-    lhs = jnp.concatenate(
-        [
-            jnp.concatenate([F3[k + t, c : c + 16, :] for t in range(4)], 1)
-            for k, c in places
-        ],
-        0,
-    )
-    y = dot(lhs, wp2[...])
-    for j in range(2):
-        skip = jnp.concatenate([x[k + j, c : c + 16, :] for k, c in places], 0)
-        mixed = mix(y[:, CH * j : CH * (j + 1)] + bias2, skip)
-        for i, (k, c) in enumerate(places):
-            out[0, k + j, c : c + 16, :] = mixed[16 * i : 16 * (i + 1)]
+    finish([(k, a, a + 16) for k in range(0, R, 2) for a in (0, C - 16)])
 
     def corner_cell(face, edge, j, at):
         e = 2 * face + edge
@@ -487,6 +515,11 @@
                 at = jnp.where(turn == 1, 3 - at, at)
                 EXT[2 * e + depth, pl.ds(1 + (R + 1) * s, 1), :] = corner_cell(g, ge, ge, at)
 
+        for t in range(2):
+            k = 2 + (R - 2) * s + t
+            patch(X3, k, 0, 0, EXT[0, pl.ds(k, 1), :], 0)
+            patch(X3, k, C - 16, 2, EXT[2, pl.ds(k, 1), :], 15)
+
         near_rows = pl.ds(1 + (R - 1) * s, 10)
         strip = jnp.concatenate(
             [
@@ -508,14 +541,14 @@
         put3(F3, 1 + (R - 1) * s, y[C : 2 * C].astype(bf16))
         patch(F3, 1 + (R - 1) * s, 0, 0, y[2 * C : 2 * C + 1], 0)
         patch(F3, 1 + (R - 1) * s, C - 16, 2, y[2 * C + 8 : 2 * C + 9], 15)
-        outer_rows(s)
-
-    @pl.loop(1, NF)
-    def _(o):
-        col_copy(o, f).wait_send()
-
-    @pl.when(r < NR - 1)
-    def _():
+        finish([((R - 2) * s, 0, C)])
+
+    @pl.when(jnp.logical_not(bottom))
+    def _():
+        @pl.loop(1, NF)
+        def _(o):
+            col_copy(o, f).wait_send()
+
         row_copy(0).wait_send()
         sel_copy(0).wait_send()
 
@@ -529,6 +562,16 @@
         @pl.loop(0, NF)
         def _(m):
             piece_copy(m, h).wait_send()
+
+    @pl.when(bottom)
+    def _():
+        to_relay().wait_send()
+
+    @pl.when(relay)
+    def _():
+        @pl.loop(1, NF)
+        def _(o):
+            relay_copy(o).wait_send()
 
     @pl.when(middle)
     def _():
@@ -551,7 +594,7 @@
     dma = pltpu.SemaphoreType.DMA
     return pl.pallas_call(
         kernel,
-        out_shape=jax.ShapeDtypeStruct((1, R, C, CH), bf16),
+        out_shape=pltpu.VMEM((1, R, C, CH), bf16),
         in_specs=[smem, smem, hbm, hbm, vmem, hbm, vmem, vmem, hbm, vmem, hbm, vmem],
         out_specs=vmem,
         scratch_shapes=[
@@ -563,6 +606,8 @@
             pltpu.VMEM((R + 4, C, K3), bf16),
             pltpu.VMEM((R + 2, C, K3), bf16),
             pltpu.VMEM((3, C, K3), bf16),
+            pltpu.VMEM((R - 4, C - 32, CH), bf16),
+            pltpu.VMEM((4, R, CH), bf16),
             pltpu.VMEM((NF, 4, R, CH), bf16),
             pltpu.VMEM((2, 2, C, CH), bf16),
             pltpu.VMEM((NH, 2, PIECE, CH), bf16),
@@ -574,7 +619,7 @@
             pltpu.VMEM((4, STRIP, CH), f32),
             pltpu.VMEM((4, STRIP, CH), f32),
             pltpu.VMEM((4, SOUT, CH), f32),
-            dma((7,)), dma((NF,)), dma((NF,)), dma((2,)), dma((2,)),
+            dma((7,)), dma((1,)), dma((1,)), dma((NF,)), dma((NF,)), dma((NF,)), dma((2,)), dma((2,)),
             dma((NF,)), dma((NH,)), dma((NH,)), dma((2,)), dma((NH,)), dma((NF,)),
             dma((2,)), dma((2,)),
         ],

time: 26.8 us -> 23.9 us (0.89)
  the two profiles are of different devices: /device:TPU:6 before, /device:TPU:0 now
where the time goes in v3:
time: 23.9 us; the launch traced here: 23.7 us
  Pallas kernels  22.7 us (95%)
  local copies, waits for them, and re-layouts  0.97 us (4%)
    pallas_call x1, Pallas kernels, per_device(): pl.pallas_call(kernel, out_shape=pltpu.VMEM((1, R, C, CH), bf16), in_spec...  22.7 us
    unnamed x1, local copies, waits for them, and re-layouts  0.97 us

profile of v3, /device:TPU:0, one launch (start us, length us, event | category | flops | bytes accessed | tf_op | source)
XLA Modules:
  0.0 23.7 jit_solution(8234805813913256188)
XLA Ops:
  0.0 22.7 %shard_map.118 = bf16[1,16,256,128]{3,2,1,0:T(8,128)(2,1)S(1)} custom-call(s32[2,4,8]{2,1,0:T(4,128)} %bitcast.11, s32[2,8]{1,0:T(2,128)} %bitcast.13, bf16[1,16,256,128]{3,2,1,0:T(8,128)(2,1)} %x_hbm.1, bf16[1152,128]{1,0:T(8,128)(2,1)} %bitcast.9, f32[1,128]{1,0:T(1,128)} %bitcast.14, bf16[1152,128]{1,0:T(8,128)(2,1)} %bitcast.10, f32[1,128]{1,0:T(1,128)} %bitcast.15, ...), custom_call_target="tpu_custom_call" | custom-call | flops 3500000000 | bytes 3000000 | tf_op jit(solution)/shard_map/pallas_call | solution.py:595
  22.8 1.0 %copy.14 = bf16[1,16,256,128]{3,2,1,0:T(8,128)(2,1)} copy(bf16[1,16,256,128]{3,2,1,0:T(8,128)(2,1)S(1)} %shard_map.118) | data formatting | bytes 2097152

commit v4 on v3

--- a/solution.py
+++ b/solution.py
@@ -207,7 +207,7 @@
         to_relay().start()
 
     def send_at(point):
-        @pl.when(jnp.logical_and(jnp.minimum(3 - place, 2) == point, jnp.logical_not(bottom)))
+        @pl.when(jnp.logical_and(jnp.where(place == 3, 0, jnp.where(place == 0, 2, 1)) == point, jnp.logical_not(bottom)))
         def _():
             send_first()
 
@@ -229,8 +229,14 @@
 
     local[1].wait()
     local[2].wait()
-    conv1_pairs(range(2, R, 2))
+    conv1_pairs((2,))
     send_at(1)
+
+    @pl.loop(0, 2)
+    def _(g):
+        conv1_pairs([4 + 6 * g + 2 * i for i in range(3)])
+
+    send_at(2)
 
     for copy in local[3:]:
         copy.wait()
@@ -340,26 +346,27 @@
                 corner_copy(m, side).start()
 
     inner = C - 32
-    normed = conv2_norm([(k, 16, C - 16) for k in range(2, R - 2, 2)])
-    for i in range(R - 4):
-        NS[i] = normed[inner * i : inner * (i + 1)]
-    send_at(2)
+    half = R // 2 - 2
 
     @pl.loop(0, 2)
     def _(g):
-        rows = [(R // 2 - 2) * g + i for i in range(R // 2 - 2)]
+        normed = conv2_norm([(2 + half * g + 2 * i, 16, C - 16) for i in range(half // 2)])
+        for i in range(half):
+            NS[half * g + i] = normed[inner * i : inner * (i + 1)]
+
+    send_strips()
+
+    @pl.loop(0, 2)
+    def _(g):
+        rows = [half * g + i for i in range(half)]
         skip = jnp.concatenate([x[2 + i, 16 : C - 16, :] for i in rows], 0)
         mixed = pointwise(jnp.concatenate([NS[i] for i in rows], 0), skip)
         for q, i in enumerate(rows):
             out[0, 2 + i, 16 : C - 16, :] = mixed[inner * q : inner * (q + 1)]
 
-        @pl.when(g == jnp.where(place < 2, 1, 0))
-        def _():
-            send_strips()
-
-    @pl.when(jnp.logical_and(middle, place > 0))
-    def _():
-        send_pieces()
+        @pl.when(jnp.logical_and(middle, jnp.logical_and(place > 0, g == jnp.where(place == 1, 1, 0))))
+        def _():
+            send_pieces()
 
     @pl.when(r > 0)
     def _():

time: 23.9 us -> 20.7 us (0.87)
  the two profiles are of different devices: /device:TPU:0 before, /device:TPU:12 now
where the time goes in v4:
time: 20.7 us; the launch traced here: 20.6 us
  Pallas kernels  19.6 us (95%)
  local copies, waits for them, and re-layouts  0.97 us (5%)
    pallas_call x1, Pallas kernels, per_device(): pl.pallas_call(kernel, out_shape=pltpu.VMEM((1, R, C, CH), bf16), in_spec...  19.6 us
    unnamed x1, local copies, waits for them, and re-layouts  0.97 us

profile of v4, /device:TPU:12, one launch (start us, length us, event | category | flops | bytes accessed | tf_op | source)
XLA Modules:
  0.0 20.6 jit_solution(10998336193391732828)
XLA Ops:
  0.0 19.6 %shard_map.118 = bf16[1,16,256,128]{3,2,1,0:T(8,128)(2,1)S(1)} custom-call(s32[2,4,8]{2,1,0:T(4,128)} %bitcast.11, s32[2,8]{1,0:T(2,128)} %bitcast.13, bf16[1,16,256,128]{3,2,1,0:T(8,128)(2,1)} %x_hbm.1, bf16[1152,128]{1,0:T(8,128)(2,1)} %bitcast.9, f32[1,128]{1,0:T(1,128)} %bitcast.14, bf16[1152,128]{1,0:T(8,128)(2,1)} %bitcast.10, f32[1,128]{1,0:T(1,128)} %bitcast.15, ...), custom_call_target="tpu_custom_call" | custom-call | flops 3500000000 | bytes 3000000 | tf_op jit(solution)/shard_map/pallas_call | solution.py:602
  19.6 1.0 %copy.14 = bf16[1,16,256,128]{3,2,1,0:T(8,128)(2,1)} copy(bf16[1,16,256,128]{3,2,1,0:T(8,128)(2,1)S(1)} %shard_map.118) | data formatting | bytes 2097152

commit v5 on v4

--- a/solution.py
+++ b/solution.py
@@ -48,6 +48,7 @@
     bottom = r == NR - 1
     hot = jnp.logical_or(top, bottom)
     middle = r == 1
+    here = (f + 3) % NF
     relay = r == NR - 2
     re = jnp.where(bottom, 1, 0)
     h = 2 * f + re
@@ -121,7 +122,7 @@
             ],
             dst_ref=PB.at[slot],
             send_sem=pbS.at[m], recv_sem=pbR.at[slot],
-            device_id={"face": m, "row": 1}, device_id_type=MESH,
+            device_id={"face": (m + NF - 3) % NF, "row": 1}, device_id_type=MESH,
         )
 
     def to_relay():
@@ -310,8 +311,8 @@
             device_id=hot_device(m), device_id_type=MESH,
         )
 
-    has_corner = jnp.logical_or(f == 0, f == NF - 1)
-    side = jnp.where(f == 0, 0, 1)
+    has_corner = jnp.logical_or(here == 0, here == NF - 1)
+    side = jnp.where(here == 0, 0, 1)
 
     def order_of(o):
         return 2 * (o % NF) + o // NF
@@ -332,14 +333,14 @@
                     for j in range(2):
                         first = PB[e, j, 0:16, :].astype(f32)[0:2]
                         last = PB[e, j, PIECE - 16 : PIECE, :].astype(f32)[14:16]
-                        cells.append(jnp.where(f == 0, first, last))
+                        cells.append(jnp.where(side == 0, first, last))
                 CT[g] = jnp.concatenate(cells, 0).astype(bf16)
 
         @pl.loop(0, NH)
         def _(o):
             m = order_of(o)
             ST[m] = PB[2 * adj[0, m % 2, m // 2] + adj[1, m % 2, m // 2]]
-            chosen_copy(m, f).start()
+            chosen_copy(m, here).start()
 
             @pl.when(has_corner)
             def _():
@@ -364,7 +365,7 @@
         for q, i in enumerate(rows):
             out[0, 2 + i, 16 : C - 16, :] = mixed[inner * q : inner * (q + 1)]
 
-        @pl.when(jnp.logical_and(middle, jnp.logical_and(place > 0, g == jnp.where(place == 1, 1, 0))))
+        @pl.when(jnp.logical_and(middle, jnp.logical_and(f > 0, g == jnp.where(place < 2, 1, 0))))
         def _():
             send_pieces()
 
@@ -388,9 +389,8 @@
     @pl.when(hot)
     def _():
         conv1_pairs((R * (1 - re),))
-        finish([((R - 2) * (1 - re), 16, C - 16)])
-
-    @pl.when(jnp.logical_and(middle, place == 0))
+
+    @pl.when(jnp.logical_and(middle, f == 0))
     def _():
         send_pieces()
 
@@ -454,18 +454,31 @@
     for k in range(4):
         FS[k] = strips[SOUT * k : SOUT * (k + 1)]
 
+    edge_row = lax.broadcasted_iota(jnp.int32, (16, 2 * CH), 0)
+    first_half = lax.broadcasted_iota(jnp.int32, (16, 2 * CH), 1) < CH
+
     @pl.loop(0, R + 2)
     def _(k):
-        patch(F3, k, 0, 0, FS[0, pl.ds(k, 1), :], 0)
-        patch(F3, k, C - 16, 2, FS[3, pl.ds(k, 1), :], 15)
-        v = FS[1, pl.ds(k, 1), :]
-        patch(F3, k, 0, 1, v, 0)
-        patch(F3, k, 0, 0, v, 1)
-        v = FS[2, pl.ds(k, 1), :]
-        patch(F3, k, C - 16, 1, v, 15)
-        patch(F3, k, C - 16, 2, v, 14)
-
-    finish([(k, a, a + 16) for k in range(0, R, 2) for a in (0, C - 16)])
+        v = [FS[i, pl.ds(k, 1), :] for i in range(4)]
+        cells = F3[k, 0:16, 0 : 2 * CH].astype(f32)
+        cells = jnp.where(edge_row == 0, jnp.concatenate([v[0], v[1]], 1), cells)
+        beside = jnp.logical_and(edge_row == 1, first_half)
+        cells = jnp.where(beside, jnp.concatenate([v[1], v[1]], 1), cells)
+        F3[k, 0:16, 0 : 2 * CH] = cells.astype(bf16)
+        cells = F3[k, C - 16 : C, CH:K3].astype(f32)
+        cells = jnp.where(edge_row == 15, jnp.concatenate([v[2], v[3]], 1), cells)
+        beside = jnp.logical_and(edge_row == 14, jnp.logical_not(first_half))
+        cells = jnp.where(beside, jnp.concatenate([v[2], v[2]], 1), cells)
+        F3[k, C - 16 : C, CH:K3] = cells.astype(bf16)
+
+    @pl.when(jnp.logical_not(hot))
+    def _():
+        finish([(k, a, a + 16) for k in range(0, R, 2) for a in (0, C - 16)])
+
+    @pl.when(hot)
+    def _():
+        outer = [(k, a, a + 16) for k in range(2, R - 2, 2) for a in (0, C - 16)]
+        finish([((R - 2) * (1 - re), 0, C)] + outer)
 
     def corner_cell(face, edge, j, at):
         e = 2 * face + edge
@@ -584,7 +597,7 @@
     def _():
         @pl.loop(0, NH)
         def _(m):
-            chosen_copy(m, f).wait_send()
+            chosen_copy(m, here).wait_send()
 
             @pl.when(has_corner)
             def _():

time: 20.7 us -> 20 us (0.966)
  the two profiles are of different devices: /device:TPU:12 before, /device:TPU:0 now
where the time goes in v5:
time: 20 us; the launch traced here: 19.9 us
  Pallas kernels  18.9 us (94%)
  local copies, waits for them, and re-layouts  0.97 us (5%)
    pallas_call x1, Pallas kernels, per_device(): pl.pallas_call(kernel, out_shape=pltpu.VMEM((1, R, C, CH), bf16), in_spec...  18.9 us
    unnamed x1, local copies, waits for them, and re-layouts  0.97 us

profile of v5, /device:TPU:0, one launch (start us, length us, event | category | flops | bytes accessed | tf_op | source)
XLA Modules:
  0.0 19.9 jit_solution(12735205289288841068)
XLA Ops:
  0.0 18.9 %shard_map.118 = bf16[1,16,256,128]{3,2,1,0:T(8,128)(2,1)S(1)} custom-call(s32[2,4,8]{2,1,0:T(4,128)} %bitcast.11, s32[2,8]{1,0:T(2,128)} %bitcast.13, bf16[1,16,256,128]{3,2,1,0:T(8,128)(2,1)} %x_hbm.1, bf16[1152,128]{1,0:T(8,128)(2,1)} %bitcast.9, f32[1,128]{1,0:T(1,128)} %bitcast.14, bf16[1152,128]{1,0:T(8,128)(2,1)} %bitcast.10, f32[1,128]{1,0:T(1,128)} %bitcast.15, ...), custom_call_target="tpu_custom_call" | custom-call | flops 3500000000 | bytes 3000000 | tf_op jit(solution)/shard_map/pallas_call | solution.py:615
  18.9 1.0 %copy.14 = bf16[1,16,256,128]{3,2,1,0:T(8,128)(2,1)} copy(bf16[1,16,256,128]{3,2,1,0:T(8,128)(2,1)S(1)} %shard_map.118) | data formatting | bytes 2097152

commit v6 on v5

--- a/solution.py
+++ b/solution.py
@@ -384,15 +384,18 @@
     @pl.when(jnp.logical_not(hot))
     def _():
         conv1_pairs((0, R))
+
+    @pl.when(jnp.logical_and(middle, f == 0))
+    def _():
+        send_pieces()
+
+    @pl.when(jnp.logical_not(hot))
+    def _():
         finish([(k, 16, C - 16) for k in (0, R - 2)])
 
     @pl.when(hot)
     def _():
         conv1_pairs((R * (1 - re),))
-
-    @pl.when(jnp.logical_and(middle, f == 0))
-    def _():
-        send_pieces()
 
     @pl.when(r > 0)
     def _():

time: 20 us -> 20.1 us (level)
  no operation moved by 1% of the time
where the time goes in v6:
time: 20.1 us; the launch traced here: 19.9 us
  Pallas kernels  18.9 us (94%)
  local copies, waits for them, and re-layouts  0.97 us (5%)
    pallas_call x1, Pallas kernels, per_device(): pl.pallas_call(kernel, out_shape=pltpu.VMEM((1, R, C, CH), bf16), in_spec...  18.9 us
    unnamed x1, local copies, waits for them, and re-layouts  0.97 us

profile of v6, /device:TPU:0, one launch (start us, length us, event | category | flops | bytes accessed | tf_op | source)
XLA Modules:
  0.0 19.9 jit_solution(13638263726800901237)
XLA Ops:
  0.0 18.9 %shard_map.118 = bf16[1,16,256,128]{3,2,1,0:T(8,128)(2,1)S(1)} custom-call(s32[2,4,8]{2,1,0:T(4,128)} %bitcast.11, s32[2,8]{1,0:T(2,128)} %bitcast.13, bf16[1,16,256,128]{3,2,1,0:T(8,128)(2,1)} %x_hbm.1, bf16[1152,128]{1,0:T(8,128)(2,1)} %bitcast.9, f32[1,128]{1,0:T(1,128)} %bitcast.14, bf16[1152,128]{1,0:T(8,128)(2,1)} %bitcast.10, f32[1,128]{1,0:T(1,128)} %bitcast.15, ...), custom_call_target="tpu_custom_call" | custom-call | flops 3500000000 | bytes 3000000 | tf_op jit(solution)/shard_map/pallas_call | solution.py:618
  18.9 1.0 %copy.14 = bf16[1,16,256,128]{3,2,1,0:T(8,128)(2,1)} copy(bf16[1,16,256,128]{3,2,1,0:T(8,128)(2,1)S(1)} %shard_map.118) | data formatting | bytes 2097152
